TPU v7x, 256 devices: a whole 4x4x8 slice. The times are simulated.
256 devices in a mesh: dp: 2 (over y_lo), ctx: 8 (over x, core), tensor: 16 (over y_hi, z).
Axes of the slice: x: 4, y: 4 (y_hi: 2, y_lo: 2; y = y_hi * 2 + y_lo), z: 8, core: 2. Of those that a mesh axis runs over, the one named last changes fastest.
Arguments:
- tokens: bfloat16 [4096, 4096], P(('dp', 'ctx', 'tensor')), parts along dimension 0, may hold values from -6 to 6
- norm_gain: float32 [4096], replicated, may hold values from 0.1 to 1.9
- in_weight: bfloat16 [4096, 3, 4096], P(None, None, 'tensor'), may hold values from -0.09375 to 0.09375
- short_filter: bfloat16 [3, 3, 4096], P(None, None, 'tensor'), may hold values from -3.5 to 3.5
- residues: float32 [16, 4096], P(None, 'tensor'), may hold values from -0.1 to 0.1
- decay_rate: float32 [16, 4096], P(None, 'tensor'), may hold values from 0.00012207031 to 0.0333333333
- skip_gain: float32 [4096], P('tensor'), may hold values from -4 to 4
- out_weight: bfloat16 [4096, 4096], P('tensor'), may hold values from -0.09375 to 0.09375
Outputs:
- layer_out: bfloat16 [4096, 4096], P(('dp', 'ctx', 'tensor')), parts along dimension 0
There are 2 independent parts, one for each index of `dp`. A program takes and returns all parts, laid end to end along the dimension named above; an argument that names none is the same for every part. Nothing has to cross between parts.
All inputs are finite; a program needn't handle non-finite values.
Results may differ from a plain program's by a relative error of at most 0.025.
Values may be sent and summed in bfloat16 or wider, within the bound.
A program may use at most 128 MiB of HBM per device.

v0:
```python
import jax
import jax.numpy as jnp
from jax import lax
from jax.sharding import PartitionSpec as P

EPSILON = 1e-06
PRECISE = lax.Precision.HIGHEST


def shifted(value, axis, steps):
    count = lax.axis_size(axis)
    initial, last = (max(0, -steps), min(count, count - steps))
    return lax.ppermute(value, axis, [(source, source + steps) for source in range(initial, last)])


def entering(x, axis, combine, identity):
    size, mine = (lax.axis_size(axis), lax.axis_index(axis))
    everything = jax.tree.map(
        lambda part, kind: lax.all_gather(part.astype(kind), axis), x, (jnp.bfloat16, jnp.bfloat16)
    )
    start = jax.tree.map(
        lambda part, zero: jnp.broadcast_to(jnp.asarray(zero, part.dtype), part.shape), x, identity
    )

    def hop(k, before):
        reached = k < mine
        new = combine(
            before, jax.tree.map(lambda part, own: part[k].astype(own.dtype), everything, x)
        )
        return jax.tree.map(lambda a, b: jnp.where(reached, a, b), new, before)

    return lax.fori_loop(0, size, hop, start)


def rms_rows(tokens, norm_gain):
    values = tokens.astype(jnp.float32)
    spread = jnp.mean(values * values, axis=-1, keepdims=True)
    return (values * lax.rsqrt(spread + EPSILON) * norm_gain).astype(jnp.bfloat16)


def short_mix(padded, short_filter, row_count):
    tap_count = short_filter.shape[0]
    summed = jnp.zeros((row_count,) + padded.shape[1:], jnp.float32)
    for tap_index in range(tap_count):
        offset = tap_count - 1 - tap_index
        summed = summed + short_filter[tap_index].astype(jnp.float32) * padded[
            offset : offset + row_count
        ].astype(jnp.float32)
    return summed


def mode_tables(residues, decay_rate, sub_width):
    lag_axis = jnp.arange(sub_width, dtype=jnp.float32)
    powers = jnp.exp(-decay_rate[:, None, :] * lag_axis[None, :, None])
    tap_sums = jnp.sum(residues[:, None, :] * powers, axis=0)
    lag_index = (
        jnp.arange(sub_width, dtype=jnp.int32)[:, None]
        - jnp.arange(sub_width, dtype=jnp.int32)[None, :]
    )
    toeplitz = jnp.where(
        (lag_index >= 0)[:, :, None], tap_sums[jnp.maximum(lag_index, 0)], jnp.float32(0.0)
    )
    ends = powers[:, ::-1, :]
    carried = residues[:, None, :] * powers * jnp.exp(-decay_rate)[:, None, :]
    return (toeplitz, ends, carried)


def on_device(
    tokens, norm_gain, in_weight, short_filter, residues, decay_rate, skip_gain, out_weight
):
    normed = rms_rows(tokens, norm_gain)
    model_width, groups, channels = in_weight.shape
    flat_weight = in_weight.reshape(model_width, groups * channels)
    projected = jnp.dot(
        lax.all_gather(normed, "tensor", axis=0, tiled=True),
        flat_weight,
        preferred_element_type=jnp.float32,
    ).astype(jnp.bfloat16)
    tap_count = short_filter.shape[0]
    block_rows = projected.shape[0]
    earlier = shifted(projected[block_rows - (tap_count - 1) :], "ctx", 1)
    padded = jnp.concatenate([earlier, projected], axis=0)
    featured = short_mix(padded, short_filter.reshape(tap_count, groups * channels), block_rows)
    featured = featured.reshape(block_rows, groups, channels)
    signal = featured[:, 0, :] * featured[:, 2, :]
    sub_width = min(128, block_rows)
    pieces = block_rows // sub_width
    toeplitz, ends, carried = mode_tables(residues, decay_rate, sub_width)
    step_decay = jnp.exp(-decay_rate * sub_width)
    blocks = signal.reshape(pieces, sub_width, channels)
    within = jnp.einsum("tsc,bsc->btc", toeplitz, blocks, precision=PRECISE)
    ends_local = jnp.einsum("msc,bsc->bmc", ends, blocks, precision=PRECISE)

    def advance(carry_state, piece_end):
        return (step_decay * carry_state + piece_end, carry_state)

    block_end, before = lax.scan(advance, jnp.zeros_like(step_decay), ends_local)
    block_decay = jnp.exp(-decay_rate * block_rows)

    def combine(earlier_pair, later_pair):
        return (earlier_pair[0] * later_pair[0], later_pair[0] * earlier_pair[1] + later_pair[1])

    prefix = entering(
        (block_decay, block_end),
        "ctx",
        combine,
        (jnp.ones_like(block_decay), jnp.zeros_like(block_end)),
    )
    incoming = prefix[1]
    piece_index = jnp.arange(pieces, dtype=jnp.float32)
    lead_decay = jnp.exp(-decay_rate[None, :, :] * (sub_width * piece_index)[:, None, None])
    prior_states = before + lead_decay * incoming[None]
    carried_in = jnp.einsum("mtc,bmc->btc", carried, prior_states, precision=PRECISE)
    long_out = (within + carried_in).reshape(block_rows, channels)
    gated_rows = (featured[:, 1, :] * (long_out + skip_gain * signal)).astype(jnp.bfloat16)
    summed = lax.psum_scatter(
        jnp.dot(gated_rows, out_weight, preferred_element_type=jnp.float32).astype(jnp.bfloat16),
        "tensor",
        scatter_dimension=0,
        tiled=True,
    ).astype(jnp.float32)
    return (summed + tokens.astype(jnp.float32)).astype(jnp.bfloat16)


def solution(mesh):
    in_specs = (
        P(("dp", "ctx", "tensor"), None),
        P(),
        P(None, None, "tensor"),
        P(None, None, "tensor"),
        P(None, "tensor"),
        P(None, "tensor"),
        P("tensor"),
        P("tensor", None),
    )
    out_specs = P(("dp", "ctx", "tensor"), None)
    return jax.shard_map(
        on_device, mesh=mesh, in_specs=in_specs, out_specs=out_specs, check_vma=False
    )
```

profile of v0, /device:TPU:2, one launch (start us, length us, event | category | flops | bytes accessed | tf_op | source)
XLA Modules:
  0.0 479.4 jit_solution(9480055802466588786)
XLA Ops:
  6.5 1.2 fusion.15
  7.7 1.7 fusion.17
  9.5 8.8 %copy.26 = bf16[4096,3,256]{0,2,1:T(8,128)(2,1)} copy(bf16[4096,3,256]{2,0,1:T(8,128)(2,1)} %param.14) | data formatting | bytes 12582912 | tf_op args[2]
  20.4 2.9 multiply_exponential_fusion
  23.3 75.1 %all-gather.4.cloned.1.call-done = bf16[256,4096]{1,0:T(8,128)(2,1)} async-done(((bf16[16,4096]{1,0:T(8,128)(2,1)}), bf16[256,4096]{1,0:T(8,128)(2,1)}) %all-gather.4.cloned.1.call-update) | async-done | bytes 2097168 | tf_op jit(solution)/shard_map/all_gather | solution.py:75
  98.4 5.2 %convolution_convert_fusion.1 = bf16[256,768]{1,0:T(8,128)(2,1)S(1)} fusion(bf16[256,4096]{1,0:T(8,128)(2,1)} %all-gather.4.cloned.1.call-done, bf16[4096,768]{0,1:T(8,128)(2,1)} %bitcast.58), kind=kOutput, calls=%fused_computation.16 | convolution fusion | flops 1610809344 | bytes 8781824 | tf_op jit(solution)/shard_map/dot_general | solution.py:74
  103.7 1.9 collective-permute-start
  105.7 12.8 %all-gather = bf16[128,256]{1,0:T(8,128)(2,1)S(1)} all-gather(bf16[16,256]{1,0:T(8,128)(2,1)S(1)} %get-tuple-element.205), channel_id=2, replica_groups=mesh['dp'=2,'ctx'=8,'tensor'=16] {'ctx'}, dimensions={0}, use_global_device_ids=true | all-gather | bytes 73728 | tf_op jit(solution)/shard_map/all_gather | solution.py:19
  118.5 4.1 rev.3
  122.7 62.0 %gather_fusion = f32[16384,256]{1,0:T(8,128)} fusion(f32[128,256]{1,0:T(8,128)S(1)} %copy.30, s32[16384]{0:T(1024)S(1)} %bitcast_clamp_fusion), kind=kCustom, calls=%fused_computation | custom fusion | bytes 33619968 | tf_op jit(solution)/shard_map/gather | solution.py:61
  184.7 18.1 %copy.31 = f32[128,128,256]{1,0,2:T(8,128)} copy(f32[128,128,256]{2,1,0:T(8,128)} %bitcast.57) | data formatting | bytes 33554432 | tf_op jit(solution)/shard_map/gather | solution.py:61
  203.5 1.2 multiply_add_fusion
  204.7 1.4 copy.27
  206.3 5.6 %convolution_bitcast_fusion = f32[2,16,256]{1,0,2:T(2,128)} fusion(f32[2,128,256]{1,0,2:T(2,128)S(1)} %mul.159, f32[16,128,256]{1,0,2:T(8,128)} %rev.3), kind=kOutput, calls=%fused_computation.18 | convolution fusion | flops 12582912 | bytes 2392064 | tf_op jit(solution)/shard_map/msc,bsc->bmc/dot_general | solution.py:92
  211.9 1.0 copy.32
  213.0 1.2 while.27
  214.2 14.0 %all-gather.1 = bf16[128,256]{1,0:T(8,128)(2,1)} all-gather(bf16[16,256]{1,0:T(8,128)(2,1)S(1)} %convert_element_type.100), channel_id=3, replica_groups=mesh['dp'=2,'ctx'=8,'tensor'=16] {'ctx'}, dimensions={0}, use_global_device_ids=true | all-gather | bytes 73728 | tf_op jit(solution)/shard_map/all_gather | solution.py:19
  228.3 5.6 %while.28 = (s32[]{:T(128)}, f32[16,256]{1,0:T(8,128)S(1)}, s32[]{:T(128)}, bf16[8,16,256]{2,1,0:T(8,128)(2,1)S(1)}, bf16[8,16,256]{2,1,0:T(8,128)(2,1)}, /*index=5*/s32[]{:T(128)}, s32[]{:T(128)}) while((s32[]{:T(128)}, f32[16,256]{1,0:T(8,128)S(1)}, s32[]{:T(128)}, bf16[8,16,256]{2,1,0:T(8,128)(2,1)S(1)}, ...), condition=%wide.region_5.6_spmd.clone, body=%wide.region_4.5_spmd.clone.sunk | while | flops 24580 | bytes 49253 | solution.py:32
  233.9 0.8 multiply_add_fusion.1
  235.6 28.7 %fusion.1 = f32[256,2,128]{2,1,0:T(2,128)S(1)} fusion(f32[2,128,256]{1,0,2:T(2,128)S(1)} %mul.159, f32[128,128,256]{1,0,2:T(8,128)} %copy.31, pred[128,128]{1,0:T(8,128)(4,1)} %subtract_compare_fusion), kind=kOutput, calls=%fused_computation.6 | convolution fusion | flops 104857600 | bytes 17317888 | tf_op jit(solution)/shard_map/tsc,bsc->btc/dot_general | solution.py:91
  264.3 3.8 fusion.8
  268.1 2.2 convolution_convert_fusion
  270.3 200.6 %reduce-scatter.2.cloned.1.call-done = bf16[16,4096]{1,0:T(8,128)(2,1)} async-done(((bf16[256,4096]{1,0:T(8,128)(2,1)}), bf16[16,4096]{1,0:T(8,128)(2,1)}) %reduce-scatter.2.cloned.1.call-update) | async-done | bytes 131088 | tf_op jit(solution)/shard_map/reduce_scatter | solution.py:116
  471.0 1.6 fusion.18
  (64 shorter events, 10.9 us)
Async XLA Ops:
  6.5 261.6 %copy-start = (bf16[256,4096]{1,0:T(8,128)(2,1)S(1)}, bf16[256,4096]{1,0:T(8,128)(2,1)}, u32[]{:S(2)}) copy-start(bf16[256,4096]{1,0:T(8,128)(2,1)} %param.19) | copy-start | bytes 6291460
  6.5 91.9 %all-gather.4.cloned.1.call-start = ((), (), s32[]{:S(2)}) async-start(), calls=%async_computation.1 | async-start | bytes 2228224 | tf_op jit(solution)/shard_map/all_gather | solution.py:75
  9.4 8.9 %copy-start.10 = (f32[16,256]{1,0:T(8,128)S(1)}, f32[16,256]{1,0:T(8,128)}, u32[]{:S(2)}) copy-start(f32[16,256]{1,0:T(8,128)} %param.17) | copy-start | bytes 49156
  9.4 9.6 %copy-start.9 = (f32[16,256]{1,0:T(8,128)S(1)}, f32[16,256]{1,0:T(8,128)}, u32[]{:S(2)}) copy-start(f32[16,256]{1,0:T(8,128)} %param.16) | copy-start | bytes 49156
  9.5 10.9 %copy-start.11 = (bf16[3,3,256]{2,1,0:T(4,128)(2,1)S(1)}, bf16[3,3,256]{2,1,0:T(4,128)(2,1)}, u32[]{:S(2)}) copy-start(bf16[3,3,256]{2,1,0:T(4,128)(2,1)} %param.15) | copy-start | bytes 13828
  9.5 461.5 %reduce-scatter.2.cloned.1.call-start = ((), (), s32[]{:S(2)}) async-start(), calls=%async_computation.2 | async-start | bytes 2228224 | tf_op jit(solution)/shard_map/reduce_scatter | solution.py:116
  18.3 0.6 copy-start.7
  19.0 84.7 %copy-start.2 = (f32[16,256]{0,1:T(8,128)}, f32[16,256]{0,1:T(8,128)S(1)}, u32[]{:S(2)}) copy-start(f32[16,256]{0,1:T(8,128)S(1)} %copy.29) | copy-start | bytes 49156
  19.2 84.5 %copy-start.4 = (f32[16,256]{0,1:T(8,128)}, f32[16,256]{0,1:T(8,128)S(1)}, u32[]{:S(2)}) copy-start(f32[16,256]{0,1:T(8,128)S(1)} %copy.28) | copy-start | bytes 49156
  103.7 99.8 %collective-permute-start = (bf16[2,768]{1,0:T(2,128)(2,1)S(1)}, bf16[2,768]{1,0:T(2,128)(2,1)S(1)}, u32[]{:S(2)}, u32[]{:S(2)}) collective-permute-start(bf16[2,768]{1,0:T(2,128)(2,1)S(1)} %slice.41), channel_id=1, source_target_pairs={{0,16},{16,32},{32,48},{48,64},{64,80},{80,96},{96,112},{1,17},{17... | collective-permute-start | bytes 9224 | tf_op jit(solution)/shard_map/ppermute | solution.py:13
  235.6 28.7 %copy-start.3 = (f32[16,256]{0,1:T(8,128)S(1)}, f32[16,256]{0,1:T(8,128)}, u32[]{:S(2)}) copy-start(f32[16,256]{0,1:T(8,128)} %copy-done.2) | copy-start | bytes 49156
  235.6 28.7 %copy-start.5 = (f32[16,256]{0,1:T(8,128)S(1)}, f32[16,256]{0,1:T(8,128)}, u32[]{:S(2)}) copy-start(f32[16,256]{0,1:T(8,128)} %copy-done.4) | copy-start | bytes 49156
  235.6 28.7 %copy-start.6 = (f32[2,16,256]{1,0,2:T(2,128)S(1)}, f32[2,16,256]{1,0,2:T(2,128)}, u32[]{:S(2)}) copy-start(f32[2,16,256]{1,0,2:T(2,128)} %copy.34) | copy-start | bytes 98308
  235.6 28.7 %copy-start.8 = (f32[16,256]{0,1:T(8,128)S(1)}, f32[16,256]{0,1:T(8,128)}, u32[]{:S(2)}) copy-start(f32[16,256]{0,1:T(8,128)} %copy.33) | copy-start | bytes 49156
  264.3 3.8 copy-start.12
  270.3 200.7 %copy-start.1 = (bf16[16,4096]{1,0:T(8,128)(2,1)S(1)}, bf16[16,4096]{1,0:T(8,128)(2,1)}, u32[]{:S(2)}) copy-start(bf16[16,4096]{1,0:T(8,128)(2,1)} %param.12) | copy-start | bytes 393220
Sparse Core Ops, SparseCore 0:
  9.9 88.4 all-gather.3
  270.4 200.4 reduce-scatter.1
where the time goes:
time: 481 us; the launch traced here: 479 us
  waiting for transfers between devices  276 us (57%)
  local copies, waits for them, and re-layouts  98.1 us (20%)
  matrix products  45.5 us (9%)
  blocking collectives  26.8 us (6%)
  other arithmetic  17.6 us (4%)
  between operations  13.6 us (3%)
    reduce_scatter x1, waiting for transfers between devices, on_device(): lax.psum_scatter(jnp.dot(gated_rows, out_weight, preferred_element_type=j...  201 us
    gather x2, local copies, waits for them, and re-layouts, mode_tables(): tap_sums[jnp.maximum(lag_index, 0)]  80.1 us
    all_gather x1, waiting for transfers between devices, on_device(): lax.all_gather(normed, 'tensor', axis=0, tiled=True)  75.1 us
    dot_general x1, matrix products, on_device(): within = jnp.einsum('tsc,bsc->btc', toeplitz, blocks, precision=PRECISE)  28.7 us
    all_gather x2, blocking collectives, entering(): lax.all_gather(part.astype(kind), axis)  26.8 us
    unnamed x29, local copies, waits for them, and re-layouts  10.6 us
  transfers between devices with their start and end apart: 3, of which 2 were waited for; matrix products, arithmetic and copies ran while one was open for 20% of the time, Pallas kernels for 0%

commit v1 on v0

v1 whole, which is shorter than its diff:
```python
import functools

import jax
import jax.numpy as jnp
from jax import lax
from jax.experimental import pallas as pl
from jax.experimental.pallas import tpu as pltpu
from jax.sharding import PartitionSpec as P

EPSILON = 1e-06
MESH = pl.DeviceIdType.MESH
SLICES = 4
SEGMENTS = 8
OWN = {(0, j): j - 1 for j in (1, 2, 3, 4)} | {(1, j): 3 + j for j in (1, 2, 3)}
OTH = {(0, j): 7 + j for j in (1, 2, 3, 4)} | {(1, j): 11 + j for j in (1, 2, 3)}
CROSS = 7
SLOTS = 15
REACH = (4, 3)


def kernel(
    sizes,
    tokens_hbm, gain_hbm, win_hbm, taps_hbm, res_hbm, rate_hbm, skip_hbm, wout_hbm,
    out_hbm,
    tok, gain, win, taps, res, rate, skip, wout,
    xg, proj, halo, sig, gate, dec, res3, far, step3, ends, state, states, inc,
    gated32, gated, part, land, outv,
    load_sem, ag_send, ag_recv, rs_send, rs_recv, halo_send, halo_recv, st_send, st_recv, out_sem,
):
    ring, n_ctx, rows, width = sizes
    block_rows = 2 * ring * rows
    cols = width // SLICES
    seg = block_rows // SEGMENTS
    channels = rate.shape[1]

    dp, ctx, tensor = lax.axis_index("dp"), lax.axis_index("ctx"), lax.axis_index("tensor")
    plane, z = tensor // ring, tensor % ring

    def at(ctx_now, plane_now, z_now):
        return (dp, ctx_now, plane_now * ring + z_now)

    partner = at(ctx, 1 - plane, z)

    loads = [
        pltpu.make_async_copy(source, target, load_sem.at[i])
        for i, (source, target) in enumerate(
            (
                (tokens_hbm, tok), (gain_hbm, gain), (rate_hbm, rate), (res_hbm, res),
                (taps_hbm, taps), (skip_hbm, skip), (win_hbm, win), (wout_hbm, wout),
            )
        )
    ]
    for load in loads:
        load.start()

    barrier = pltpu.get_barrier_semaphore()
    peers = [partner, at(ctx, plane, (z + 1) % ring), at(ctx, plane, (z + ring - 1) % ring)]
    peers += [at((ctx + o) % n_ctx, plane, z) for o in range(1, n_ctx)]
    for peer in peers:
        pl.semaphore_signal(barrier, inc=1, device_id=peer, device_id_type=MESH)

    def ring_at(k, chain, steps):
        sign = 1 - 2 * (k % 2) if chain == 0 else 2 * (k % 2) - 1
        return (z + sign * steps + 2 * ring) % ring

    def block(plane_now, z_now):
        return pl.ds(pl.multiple_of((plane_now * ring + z_now) * rows, rows), rows)

    def gather_copy(k, slot, plane_now, z_now, target):
        where = xg.at[k, block(plane_now, z_now), :]
        return pltpu.make_async_remote_copy(
            src_ref=where, dst_ref=where, send_sem=ag_send.at[k, slot], recv_sem=ag_recv.at[k, slot],
            device_id=target, device_id_type=MESH,
        )

    def scatter_copy(k, slot, plane_now, z_now, target):
        return pltpu.make_async_remote_copy(
            src_ref=part.at[k, block(plane_now, z_now), :], dst_ref=land.at[k, slot],
            send_sem=rs_send.at[k, slot], recv_sem=rs_recv.at[k, slot],
            device_id=target, device_id_type=MESH,
        )

    def each_slice(body):
        def step(k, carry):
            body(k)
            return carry

        lax.fori_loop(0, SLICES, step, 0)

    loads[0].wait()
    loads[1].wait()
    values = tok[...].astype(jnp.float32)
    spread = jnp.mean(values * values, axis=-1, keepdims=True)
    normed = (values * lax.rsqrt(spread + EPSILON) * gain[...]).astype(jnp.bfloat16)
    for k in range(SLICES):
        xg[k, block(plane, z), :] = normed[:, k * cols : (k + 1) * cols]
    pl.semaphore_wait(barrier, len(peers))

    def start_own(k):
        gather_copy(k, OWN[0, 1], plane, z, at(ctx, plane, ring_at(k, 0, 1))).start()
        gather_copy(k, OWN[1, 1], plane, z, at(ctx, plane, ring_at(k, 1, 1))).start()
        gather_copy(k, CROSS, plane, z, partner).start()

    each_slice(start_own)

    loads[2].wait()
    loads[3].wait()
    loads[4].wait()
    loads[5].wait()
    modes = rate.shape[0]
    for m in range(modes):
        step3[m] = jnp.broadcast_to(rate[m : m + 1, :], (SEGMENTS, channels))
        res3[m] = jnp.broadcast_to(res[m : m + 1, :], (SEGMENTS, channels))
    dec[...] = jnp.exp(-step3[...])

    def pass_own(j, chain):
        def body(k):
            origin = ring_at(k, chain, -j)
            gather_copy(k, OWN[chain, j], plane, origin, partner).wait_recv()
            gather_copy(k, OWN[chain, j + 1], plane, origin, at(ctx, plane, ring_at(k, chain, 1))).start()
            if j <= 2:
                gather_copy(k, OTH[chain, j], plane, origin, partner).start()

        return body

    def pass_other(j, chain):
        def body(k):
            origin = ring_at(k, chain, -j)
            gather_copy(k, OTH[chain, j], 1 - plane, origin, partner).wait_recv()
            gather_copy(k, OTH[chain, j + 1], 1 - plane, origin, at(ctx, plane, ring_at(k, chain, 1))).start()

        return body

    def both(*bodies):
        def body(k):
            for one in bodies:
                one(k)

        return body

    each_slice(both(pass_own(1, 0), pass_own(1, 1)))
    each_slice(both(pass_own(2, 0), pass_own(2, 1)))
    each_slice(both(pass_other(2, 0), pass_other(2, 1)))
    each_slice(both(pass_own(3, 0), pass_other(3, 0)))

    loads[6].wait()

    def project(k):
        for slot, plane_now, origin in (
            (OWN[1, 3], plane, ring_at(k, 1, -3)),
            (OTH[1, 3], 1 - plane, ring_at(k, 1, -3)),
            (OWN[0, 4], plane, ring_at(k, 0, -4)),
            (OTH[0, 4], 1 - plane, ring_at(k, 0, -4)),
            (CROSS, 1 - plane, z),
            (OTH[0, 1], 1 - plane, ring_at(k, 0, -1)),
            (OTH[1, 1], 1 - plane, ring_at(k, 1, -1)),
        ):
            gather_copy(k, slot, plane_now, origin, partner).wait_recv()
        depth = pl.ds(pl.multiple_of(k * cols, cols), cols)
        for g in range(3):
            group = pl.ds(g * channels, channels)
            product = jnp.dot(xg[k], win[g, depth, :], preferred_element_type=jnp.float32)
            product = product.reshape(SEGMENTS, seg, channels)

            @pl.when(k == 0)
            def _():
                proj[:, :, group] = product

            @pl.when(k > 0)
            def _():
                proj[:, :, group] += product

    each_slice(project)

    halo_copy = pltpu.make_async_remote_copy(
        src_ref=proj.at[SEGMENTS - 1, pl.ds(seg - 8, 8), :], dst_ref=halo,
        send_sem=halo_send, recv_sem=halo_recv,
        device_id=at((ctx + 1) % n_ctx, plane, z), device_id_type=MESH,
    )
    halo_copy.start()
    taps32 = taps[...].astype(jnp.float32)

    def short_mix(i, now, one, two):
        featured = []
        for g in range(3):
            group = slice(g * channels, (g + 1) * channels)
            featured.append(
                taps32[0, g : g + 1, :] * now[:, group]
                + taps32[1, g : g + 1, :] * one[:, group]
                + taps32[2, g : g + 1, :] * two[:, group]
            )
        sig[i] = featured[0] * featured[2]
        gate[i] = featured[1]

    def short_step(i, carry):
        short_mix(i, proj[:, i, :], proj[:, i - 1, :], proj[:, i - 2, :])
        return carry

    lax.fori_loop(2, seg, short_step, 0)

    halves = [pl.ds(first, 128) for first in range(0, channels, 128)]
    for half in halves:

        def end_step(i, carry, half=half):
            return dec[:, :, half] * carry + sig[i, :, half][None]

        ends[:, :, half] = lax.fori_loop(2, seg, end_step, jnp.zeros((modes, SEGMENTS, 128), jnp.float32))
    far[...] = jnp.exp(step3[...] * (-float(seg - 2)))

    halo_copy.wait_recv()
    first_row = lax.broadcasted_iota(jnp.int32, (SEGMENTS, 3 * channels), 0) == 0
    first_block = ctx == 0

    def entering(row, last):
        before = jnp.where(first_block, 0.0, halo[row : row + 1, :])
        return jnp.where(first_row, jnp.broadcast_to(before, last.shape), pltpu.roll(last, 1, 0))

    row_one = entering(7, proj[:, seg - 1, :])
    row_two = entering(6, proj[:, seg - 2, :])
    row_zero = proj[:, 0, :]
    short_mix(0, row_zero, row_one, row_two)
    short_mix(1, proj[:, 1, :], row_zero, row_one)

    lane = lax.broadcasted_iota(jnp.int32, (modes, SEGMENTS, 128), 1)
    for half in halves:
        total = ends[:, :, half] + far[:, :, half] * (dec[:, :, half] * sig[0, :, half][None] + sig[1, :, half][None])
        leap = far[:, :, half] * dec[:, :, half] * dec[:, :, half]
        for hop in (1, 2, 4):
            moved = pltpu.roll(total, hop, 1)
            total = total + jnp.where(lane >= hop, leap * moved, 0.0)
            leap = leap * leap
        ends[:, :, half] = total
    state[...] = ends[:, SEGMENTS - 1, :].astype(jnp.bfloat16)
    state_copies = [
        pltpu.make_async_remote_copy(
            src_ref=state, dst_ref=states.at[o - 1], send_sem=st_send.at[o - 1], recv_sem=st_recv.at[o - 1],
            device_id=at((ctx + o) % n_ctx, plane, z), device_id_type=MESH,
        )
        for o in range(1, n_ctx)
    ]
    for copy in state_copies:
        copy.start()
    segment = lax.broadcasted_iota(jnp.int32, (modes, SEGMENTS, channels), 1)
    step3[...] = jnp.exp(step3[...] * (segment.astype(jnp.float32) * (-float(seg))))
    for half in halves:
        ends[:, :, half] = jnp.where(lane >= 1, pltpu.roll(ends[:, :, half], 1, 1), 0.0)
    block_decay = jnp.exp(rate[...] * (-float(block_rows)))
    incoming = jnp.zeros(rate.shape, jnp.float32)
    for o in range(n_ctx - 1, 0, -1):
        state_copies[o - 1].wait_recv()
        incoming = block_decay * incoming + jnp.where(o <= ctx, states[o - 1].astype(jnp.float32), 0.0)
    inc[...] = incoming
    for m in range(modes):
        ends[m] = ends[m] + step3[m] * inc[m : m + 1, :]

    for half in halves:

        def long_step(i, carry, half=half):
            now = sig[i, :, half]
            carry = dec[:, :, half] * carry + now[None]
            mixed = jnp.sum(res3[:, :, half] * carry, axis=0)
            gated32[i, :, half] = gate[i, :, half] * (mixed + skip[:, half] * now)
            return carry

        lax.fori_loop(0, seg, long_step, ends[:, :, half])
    for s in range(SEGMENTS):
        gated[s * seg : (s + 1) * seg, :] = gated32[:, s, :].astype(jnp.bfloat16)

    loads[7].wait()

    def send_along(k, chain, j, plane_now, table):
        target = at(ctx, plane, ring_at(k, chain, -1))
        scatter_copy(k, table[chain, j], plane_now, ring_at(k, chain, -j), target).start()

    def send_across(k, chain, j):
        scatter_copy(k, OTH[chain, j], 1 - plane, ring_at(k, chain, -j), partner).start()

    def add(k, plane_now, z_now, slots):
        where = block(plane_now, z_now)
        total = part[k, where, :].astype(jnp.float32)
        for slot in slots:
            scatter_copy(k, slot, plane_now, z_now, partner).wait_recv()
            total = total + land[k, slot].astype(jnp.float32)
        part[k, where, :] = total.astype(jnp.bfloat16)

    def multiply(k):
        depth = pl.ds(pl.multiple_of(k * cols, cols), cols)
        part[k] = jnp.dot(gated[...], wout[:, depth], preferred_element_type=jnp.float32).astype(jnp.bfloat16)
        send_along(k, 0, 4, plane, OWN)
        send_along(k, 0, 4, 1 - plane, OTH)
        send_along(k, 1, 3, 1 - plane, OTH)
        send_along(k, 1, 3, plane, OWN)
        scatter_copy(k, CROSS, 1 - plane, z, partner).start()
        send_across(k, 0, 1)
        send_across(k, 1, 1)

    each_slice(multiply)

    def reduce_three(k):
        add(k, 1 - plane, ring_at(k, 0, -3), [OTH[0, 4]])
        send_along(k, 0, 3, 1 - plane, OTH)
        add(k, plane, ring_at(k, 0, -3), [OWN[0, 4]])
        send_along(k, 0, 3, plane, OWN)

    each_slice(reduce_three)

    def cross_two(k):
        for chain in (1, 0):
            add(k, 1 - plane, ring_at(k, chain, -2), [OTH[chain, 3]])
            send_across(k, chain, 2)

    each_slice(cross_two)

    def reduce_two(k):
        for chain in (1, 0):
            add(k, plane, ring_at(k, chain, -2), [OWN[chain, 3], OTH[chain, 2]])
            send_along(k, chain, 2, plane, OWN)

    each_slice(reduce_two)

    def reduce_one(k):
        for chain in (1, 0):
            add(k, plane, ring_at(k, chain, -1), [OTH[chain, 1], OWN[chain, 2]])
            send_along(k, chain, 1, plane, OWN)

    each_slice(reduce_one)

    for k in range(SLICES):
        total = part[k, block(plane, z), :].astype(jnp.float32)
        for slot in (CROSS, OWN[0, 1], OWN[1, 1]):
            scatter_copy(k, slot, plane, z, partner).wait_recv()
            total = total + land[k, slot].astype(jnp.float32)
        total = total + tok[:, k * cols : (k + 1) * cols].astype(jnp.float32)
        outv[:, k * cols : (k + 1) * cols] = total.astype(jnp.bfloat16)
    write = pltpu.make_async_copy(outv, out_hbm, out_sem)
    write.start()

    def drain(k):
        for slot in range(SLOTS):
            gather_copy(k, slot, plane, z, partner).wait_send()
            scatter_copy(k, slot, plane, z, partner).wait_send()

    each_slice(drain)
    halo_copy.wait_send()
    for copy in state_copies:
        copy.wait_send()
    write.wait()


def on_device(ring, n_ctx, tokens, norm_gain, in_weight, short_filter, residues, decay_rate, skip_gain, out_weight):
    rows, width = tokens.shape
    modes, channels = decay_rate.shape
    block_rows = 2 * ring * rows
    seg = block_rows // SEGMENTS
    cols = width // SLICES
    f32, bf16 = jnp.float32, jnp.bfloat16
    any_spec = pl.BlockSpec(memory_space=pl.ANY)
    table = pltpu.VMEM((modes, SEGMENTS, channels), f32)
    dma = pltpu.SemaphoreType.DMA
    return pl.pallas_call(
        functools.partial(kernel, (ring, n_ctx, rows, width)),
        out_shape=jax.ShapeDtypeStruct((rows, width), bf16),
        in_specs=[any_spec] * 8,
        out_specs=any_spec,
        scratch_shapes=[
            pltpu.VMEM((rows, width), bf16),
            pltpu.VMEM((1, width), f32),
            pltpu.VMEM((3, width, channels), bf16),
            pltpu.VMEM(short_filter.shape, bf16),
            pltpu.VMEM((modes, channels), f32),
            pltpu.VMEM((modes, channels), f32),
            pltpu.VMEM((1, channels), f32),
            pltpu.VMEM((channels, width), bf16),
            pltpu.VMEM((SLICES, block_rows, cols), bf16),
            pltpu.VMEM((SEGMENTS, seg, 3 * channels), f32),
            pltpu.VMEM((8, 3 * channels), f32),
            pltpu.VMEM((seg, SEGMENTS, channels), f32),
            pltpu.VMEM((seg, SEGMENTS, channels), f32),
            table, table, table, table, table,
            pltpu.VMEM((modes, channels), bf16),
            pltpu.VMEM((n_ctx - 1, modes, channels), bf16),
            pltpu.VMEM((modes, channels), f32),
            pltpu.VMEM((seg, SEGMENTS, channels), f32),
            pltpu.VMEM((block_rows, channels), bf16),
            pltpu.VMEM((SLICES, block_rows, cols), bf16),
            pltpu.VMEM((SLICES, SLOTS, rows, cols), bf16),
            pltpu.VMEM((rows, width), bf16),
            dma((8,)),
            dma((SLICES, SLOTS)), dma((SLICES, SLOTS)),
            dma((SLICES, SLOTS)), dma((SLICES, SLOTS)),
            dma, dma,
            dma((n_ctx - 1,)), dma((n_ctx - 1,)),
            dma,
        ],
        name="hyena_layer",
        cost_estimate=pl.CostEstimate(
            flops=2 * block_rows * width * channels * 4, bytes_accessed=8 * width * channels, transcendentals=0
        ),
        compiler_params=pltpu.CompilerParams(
            collective_id=0, has_side_effects=True, vmem_limit_bytes=48 * 2**20
        ),
    )(
        tokens, norm_gain.reshape(1, width), in_weight.transpose(1, 0, 2), short_filter,
        residues, decay_rate, skip_gain.reshape(1, channels), out_weight,
    )


def solution(mesh):
    ring, n_ctx = mesh.shape["tensor"] // 2, mesh.shape["ctx"]
    in_specs = (
        P(("dp", "ctx", "tensor"), None),
        P(),
        P(None, None, "tensor"),
        P(None, None, "tensor"),
        P(None, "tensor"),
        P(None, "tensor"),
        P("tensor"),
        P("tensor", None),
    )
    out_specs = P(("dp", "ctx", "tensor"), None)
    return jax.shard_map(
        functools.partial(on_device, ring, n_ctx),
        mesh=mesh, in_specs=in_specs, out_specs=out_specs, check_vma=False,
    )
```

time: 481 us -> 75.3 us (0.16)
  waiting for transfers between devices: 276 us -> 0 us
  local copies, waits for them, and re-layouts: 98.1 us -> 6.67 us
  Pallas kernels: 0 us -> 68 us
  matrix products: 45.5 us -> 0 us
  blocking collectives: 26.8 us -> 0 us
  other arithmetic: 17.6 us -> 0 us
  between operations: 13.6 us -> 0.02 us
    reduce_scatter x1 -> x0, waiting for transfers between devices: 201 us -> none  [on_device(): lax.psum_scatter(jnp.dot(gated_rows, out_weight, preferred_element_type=j...]
    gather x2 -> x0, local copies, waits for them, and re-layouts: 80.1 us -> none  [mode_tables(): tap_sums[jnp.maximum(lag_index, 0)]]
    all_gather x1 -> x0, waiting for transfers between devices: 75.1 us -> none  [on_device(): lax.all_gather(normed, 'tensor', axis=0, tiled=True)]
    pallas_call x0 -> x1, Pallas kernels: none -> 68 us  [on_device(): pl.pallas_call(functools.partial(kernel, (ring, n_ctx, rows, width)), out...]
    dot_general x5 -> x0, matrix products: 45.5 us -> none  [the longest x1 28.7 us: on_device(): within = jnp.einsum('tsc,bsc->btc', toeplitz, blocks, precision=PRECISE)]
    all_gather x2 -> x0, blocking collectives: 26.8 us -> none  [entering(): lax.all_gather(part.astype(kind), axis)]
    select_n x8 -> x0, other arithmetic: 5.64 us -> none  [hop(): return jax.tree.map(lambda a, b: jnp.where(reached, a, b), new, before)]
    unnamed x29 -> x15, local copies, waits for them, and re-layouts: 10.6 us -> 6.67 us
  transfers between devices with their start and end apart: 3 -> 0, of which waited for: 2 -> 0; matrix products, arithmetic and copies ran while one was open for 20% -> 0% of each run, Pallas kernels for 0% -> 0%
where the time goes in v1:
time: 75.3 us; the launch traced here: 74.7 us
  Pallas kernels  68 us (90%)
  local copies, waits for them, and re-layouts  6.67 us (9%)
    pallas_call x1, Pallas kernels, on_device(): pl.pallas_call(functools.partial(kernel, (ring, n_ctx, rows, width)), out...  68 us
    unnamed x15, local copies, waits for them, and re-layouts  6.67 us

profile of v1, /device:TPU:2, one launch (start us, length us, event | category | flops | bytes accessed | tf_op | source)
XLA Modules:
  0.0 74.7 jit_solution(14275043314319079021)
XLA Ops:
  0.0 0.0 copy-start
  0.0 1.6 %copy-done = bf16[256,4096]{1,0:T(8,128)(2,1)S(1)} copy-done((bf16[256,4096]{1,0:T(8,128)(2,1)S(1)}, bf16[256,4096]{1,0:T(8,128)(2,1)}, u32[]{:S(2)}) %copy-start) | copy-done | bytes 2097176
  1.6 0.0 copy-start.1
  1.6 0.9 %copy-done.1 = bf16[16,4096]{1,0:T(8,128)(2,1)S(1)} copy-done((bf16[16,4096]{1,0:T(8,128)(2,1)S(1)}, bf16[16,4096]{1,0:T(8,128)(2,1)}, u32[]{:S(2)}) %copy-start.1) | copy-done | bytes 131096
  2.5 0.0 copy-start.2
  2.5 0.7 copy-done.2
  3.2 0.0 copy-start.3
  3.2 0.7 copy-done.3
  3.9 0.0 copy-start.4
  3.9 0.7 copy-done.4
  4.7 0.0 copy-start.5
  4.7 0.7 copy-done.5
  5.3 0.0 copy-start.6
  5.3 0.7 copy-done.6
  6.0 68.0 %hyena_layer.1 = bf16[16,4096]{1,0:T(8,128)(2,1)S(1)} custom-call(bf16[16,4096]{1,0:T(8,128)(2,1)S(1)} %copy-done.1, f32[1,4096]{1,0:T(1,128)S(1)} %bitcast.3, bf16[3,4096,256]{2,1,0:T(8,128)(2,1)} %bitcast.5, bf16[3,3,256]{2,1,0:T(4,128)(2,1)S(1)} %copy-done.5, f32[16,256]{1,0:T(8,128)S(1)} %copy-done.3, f32[16,256]{1,0:T(8,128)S(1)} %copy-done.4, ...), custom_call_target="tpu_custom_call" | custom-call | flops 2147483648 | bytes 8388608 | tf_op jit(solution)/shard_map/hyena_layer/pallas_call | solution.py:360
  74.1 0.7 copy.10
Async XLA Ops:
  0.0 1.6 %copy-start = (bf16[256,4096]{1,0:T(8,128)(2,1)S(1)}, bf16[256,4096]{1,0:T(8,128)(2,1)}, u32[]{:S(2)}) copy-start(bf16[256,4096]{1,0:T(8,128)(2,1)} %wout_hbm.1) | copy-start | bytes 6291460
  1.6 0.9 %copy-start.1 = (bf16[16,4096]{1,0:T(8,128)(2,1)S(1)}, bf16[16,4096]{1,0:T(8,128)(2,1)}, u32[]{:S(2)}) copy-start(bf16[16,4096]{1,0:T(8,128)(2,1)} %tokens_hbm.1) | copy-start | bytes 393220
  2.5 0.7 copy-start.2
  3.2 0.7 copy-start.3
  3.9 0.7 copy-start.4
  4.7 0.7 copy-start.5
  5.3 0.7 copy-start.6

commit v2 on v1

--- a/solution.py
+++ b/solution.py
@@ -113,49 +113,65 @@
         res3[m] = jnp.broadcast_to(res[m : m + 1, :], (SEGMENTS, channels))
     dec[...] = jnp.exp(-step3[...])
 
-    def pass_own(j, chain):
-        def body(k):
-            origin = ring_at(k, chain, -j)
-            gather_copy(k, OWN[chain, j], plane, origin, partner).wait_recv()
-            gather_copy(k, OWN[chain, j + 1], plane, origin, at(ctx, plane, ring_at(k, chain, 1))).start()
-            if j <= 2:
-                gather_copy(k, OTH[chain, j], plane, origin, partner).start()
-
-        return body
-
-    def pass_other(j, chain):
-        def body(k):
-            origin = ring_at(k, chain, -j)
-            gather_copy(k, OTH[chain, j], 1 - plane, origin, partner).wait_recv()
-            gather_copy(k, OTH[chain, j + 1], 1 - plane, origin, at(ctx, plane, ring_at(k, chain, 1))).start()
-
-        return body
-
-    def both(*bodies):
-        def body(k):
-            for one in bodies:
-                one(k)
-
-        return body
-
-    each_slice(both(pass_own(1, 0), pass_own(1, 1)))
-    each_slice(both(pass_own(2, 0), pass_own(2, 1)))
-    each_slice(both(pass_other(2, 0), pass_other(2, 1)))
-    each_slice(both(pass_own(3, 0), pass_other(3, 0)))
+    def arrived(k, slot, plane_now, origin):
+        gather_copy(k, slot, plane_now, origin, partner).wait_recv()
+
+    def along(k, chain, table, j, plane_now):
+        target = at(ctx, plane, ring_at(k, chain, 1))
+        gather_copy(k, table[chain, j], plane_now, ring_at(k, chain, 1 - j), target).start()
+
+    def across(k, chain, j):
+        gather_copy(k, OTH[chain, j], plane, ring_at(k, chain, -j), partner).start()
+
+    def got_own(k, chain, j):
+        arrived(k, OWN[chain, j], plane, ring_at(k, chain, -j))
+
+    def got_other(k, chain, j):
+        arrived(k, OTH[chain, j], 1 - plane, ring_at(k, chain, -j))
+
+    def gather_one(k):
+        got_own(k, 0, 1)
+        along(k, 0, OWN, 2, plane)
+        across(k, 0, 1)
+        got_own(k, 1, 1)
+        along(k, 1, OWN, 2, plane)
+
+    def gather_two(k):
+        got_own(k, 0, 2)
+        along(k, 0, OWN, 3, plane)
+        got_own(k, 1, 2)
+        along(k, 1, OWN, 3, plane)
+        across(k, 1, 2)
+
+    def gather_three(k):
+        got_own(k, 0, 3)
+        along(k, 0, OWN, 4, plane)
+        across(k, 0, 3)
+        arrived(k, CROSS, 1 - plane, z)
+        along(k, 1, OTH, 1, 1 - plane)
+        got_own(k, 1, 3)
+        across(k, 1, 3)
+
+    def gather_four(k):
+        got_other(k, 0, 1)
+        along(k, 0, OTH, 2, 1 - plane)
+
+    def gather_five(k):
+        got_other(k, 0, 3)
+        along(k, 0, OTH, 4, 1 - plane)
+
+    for body in (gather_one, gather_two, gather_three, gather_four, gather_five):
+        each_slice(body)
 
     loads[6].wait()
 
     def project(k):
-        for slot, plane_now, origin in (
-            (OWN[1, 3], plane, ring_at(k, 1, -3)),
-            (OTH[1, 3], 1 - plane, ring_at(k, 1, -3)),
-            (OWN[0, 4], plane, ring_at(k, 0, -4)),
-            (OTH[0, 4], 1 - plane, ring_at(k, 0, -4)),
-            (CROSS, 1 - plane, z),
-            (OTH[0, 1], 1 - plane, ring_at(k, 0, -1)),
-            (OTH[1, 1], 1 - plane, ring_at(k, 1, -1)),
-        ):
-            gather_copy(k, slot, plane_now, origin, partner).wait_recv()
+        got_own(k, 0, 4)
+        got_other(k, 1, 1)
+        got_other(k, 1, 2)
+        got_other(k, 0, 2)
+        got_other(k, 1, 3)
+        got_other(k, 0, 4)
         depth = pl.ds(pl.multiple_of(k * cols, cols), cols)
         for g in range(3):
             group = pl.ds(g * channels, channels)
@@ -286,44 +302,43 @@
     def multiply(k):
         depth = pl.ds(pl.multiple_of(k * cols, cols), cols)
         part[k] = jnp.dot(gated[...], wout[:, depth], preferred_element_type=jnp.float32).astype(jnp.bfloat16)
+        send_across(k, 1, 3)
+        send_along(k, 0, 4, 1 - plane, OTH)
         send_along(k, 0, 4, plane, OWN)
-        send_along(k, 0, 4, 1 - plane, OTH)
-        send_along(k, 1, 3, 1 - plane, OTH)
+        send_along(k, 1, 1, 1 - plane, OTH)
+        send_along(k, 0, 2, 1 - plane, OTH)
+
+    each_slice(multiply)
+
+    def reduce_one(k):
+        add(k, 1 - plane, ring_at(k, 0, -3), [OTH[0, 4]])
+        send_across(k, 0, 3)
+        add(k, plane, ring_at(k, 1, -3), [OTH[1, 3]])
         send_along(k, 1, 3, plane, OWN)
+        send_across(k, 1, 2)
+
+    def reduce_two(k):
+        add(k, plane, ring_at(k, 0, -3), [OWN[0, 4], OTH[0, 3]])
+        send_along(k, 0, 3, plane, OWN)
+        add(k, 1 - plane, ring_at(k, 0, -1), [OTH[0, 2]])
+        send_across(k, 0, 1)
+
+    def reduce_three(k):
+        add(k, plane, ring_at(k, 1, -2), [OWN[1, 3], OTH[1, 2]])
+        send_along(k, 1, 2, plane, OWN)
+        add(k, plane, ring_at(k, 0, -2), [OWN[0, 3]])
+        send_along(k, 0, 2, plane, OWN)
+        add(k, 1 - plane, z, [OTH[1, 1]])
         scatter_copy(k, CROSS, 1 - plane, z, partner).start()
-        send_across(k, 0, 1)
-        send_across(k, 1, 1)
-
-    each_slice(multiply)
-
-    def reduce_three(k):
-        add(k, 1 - plane, ring_at(k, 0, -3), [OTH[0, 4]])
-        send_along(k, 0, 3, 1 - plane, OTH)
-        add(k, plane, ring_at(k, 0, -3), [OWN[0, 4]])
-        send_along(k, 0, 3, plane, OWN)
-
-    each_slice(reduce_three)
-
-    def cross_two(k):
-        for chain in (1, 0):
-            add(k, 1 - plane, ring_at(k, chain, -2), [OTH[chain, 3]])
-            send_across(k, chain, 2)
-
-    each_slice(cross_two)
-
-    def reduce_two(k):
-        for chain in (1, 0):
-            add(k, plane, ring_at(k, chain, -2), [OWN[chain, 3], OTH[chain, 2]])
-            send_along(k, chain, 2, plane, OWN)
-
-    each_slice(reduce_two)
-
-    def reduce_one(k):
-        for chain in (1, 0):
-            add(k, plane, ring_at(k, chain, -1), [OTH[chain, 1], OWN[chain, 2]])
-            send_along(k, chain, 1, plane, OWN)
-
-    each_slice(reduce_one)
+
+    def reduce_four(k):
+        add(k, plane, ring_at(k, 1, -1), [OWN[1, 2]])
+        send_along(k, 1, 1, plane, OWN)
+        add(k, plane, ring_at(k, 0, -1), [OTH[0, 1], OWN[0, 2]])
+        send_along(k, 0, 1, plane, OWN)
+
+    for body in (reduce_one, reduce_two, reduce_three, reduce_four):
+        each_slice(body)
 
     for k in range(SLICES):
         total = part[k, block(plane, z), :].astype(jnp.float32)
@@ -397,7 +412,7 @@
             flops=2 * block_rows * width * channels * 4, bytes_accessed=8 * width * channels, transcendentals=0
         ),
         compiler_params=pltpu.CompilerParams(
-            collective_id=0, has_side_effects=True, vmem_limit_bytes=48 * 2**20
+            collective_id=0, has_side_effects=True, vmem_limit_bytes=64 * 2**20
         ),
     )(
         tokens, norm_gain.reshape(1, width), in_weight.transpose(1, 0, 2), short_filter,

time: 75.3 us -> 63.3 us (0.84)
  Pallas kernels: 68 us -> 61.6 us
  local copies, waits for them, and re-layouts: 6.67 us -> 1.57 us
    pallas_call x1, Pallas kernels: 68 us -> 61.6 us  [on_device(): pl.pallas_call(functools.partial(kernel, (ring, n_ctx, rows, width)), out...]
    unnamed x15 -> x1, local copies, waits for them, and re-layouts: 6.67 us -> 1.57 us
where the time goes in v2:
time: 63.3 us; the launch traced here: 63.2 us
  Pallas kernels  61.6 us (97%)
  local copies, waits for them, and re-layouts  1.57 us (2%)
    pallas_call x1, Pallas kernels, on_device(): pl.pallas_call(functools.partial(kernel, (ring, n_ctx, rows, width)), out...  61.6 us
    unnamed x1, local copies, waits for them, and re-layouts  1.57 us

profile of v2, /device:TPU:2, one launch (start us, length us, event | category | flops | bytes accessed | tf_op | source)
XLA Modules:
  0.0 63.2 jit_solution(17712068817367788195)
XLA Ops:
  0.0 61.6 %hyena_layer.1 = bf16[16,4096]{1,0:T(8,128)(2,1)} custom-call(bf16[16,4096]{1,0:T(8,128)(2,1)} %tokens_hbm.1, f32[1,4096]{1,0:T(1,128)} %bitcast.4, bf16[3,4096,256]{2,1,0:T(8,128)(2,1)} %bitcast.3, bf16[3,3,256]{2,1,0:T(4,128)(2,1)} %taps_hbm.1, f32[16,256]{1,0:T(8,128)} %res_hbm.1, f32[16,256]{1,0:T(8,128)} %rate_hbm.1, f32[1,256]{1,0:T(1,128)} %bitcast.5, ...), custom_call_target="tpu_custom_call" | custom-call | flops 2147483648 | bytes 8388608 | tf_op jit(solution)/shard_map/hyena_layer/pallas_call | solution.py:375
  61.6 1.6 %copy.10 = bf16[16,4096]{1,0:T(8,128)(2,1)} copy(bf16[16,4096]{1,0:T(8,128)(2,1)} %hyena_layer.1) | data formatting | bytes 262144

commit v3 on v2

--- a/solution.py
+++ b/solution.py
@@ -21,11 +21,11 @@
 def kernel(
     sizes,
     tokens_hbm, gain_hbm, win_hbm, taps_hbm, res_hbm, rate_hbm, skip_hbm, wout_hbm,
-    out_hbm,
+    out,
     tok, gain, win, taps, res, rate, skip, wout,
-    xg, proj, halo, sig, gate, dec, res3, far, step3, ends, state, states, inc,
-    gated32, gated, part, land, outv,
-    load_sem, ag_send, ag_recv, rs_send, rs_recv, halo_send, halo_recv, st_send, st_recv, out_sem,
+    xg, proj, sig, gate, dec, res3, far, step3, ends, message, messages, rows32, before, heads, decays, inc,
+    gated32, gated, part, land,
+    load_sem, ag_send, ag_recv, rs_send, rs_recv, st_send, st_recv,
 ):
     ring, n_ctx, rows, width = sizes
     block_rows = 2 * ring * rows
@@ -85,7 +85,7 @@
             body(k)
             return carry
 
-        lax.fori_loop(0, SLICES, step, 0)
+        lax.fori_loop(0, SLICES, step, 0, unroll=True)
 
     loads[0].wait()
     loads[1].wait()
@@ -112,6 +112,13 @@
         step3[m] = jnp.broadcast_to(rate[m : m + 1, :], (SEGMENTS, channels))
         res3[m] = jnp.broadcast_to(res[m : m + 1, :], (SEGMENTS, channels))
     dec[...] = jnp.exp(-step3[...])
+    far[...] = jnp.exp(step3[...] * (-float(seg)))
+    segment = lax.broadcasted_iota(jnp.int32, (modes, SEGMENTS, channels), 1)
+    step3[...] = jnp.exp(step3[...] * (segment.astype(jnp.float32) * (-float(seg))))
+    decays[0] = jnp.exp(-rate[...])
+    decays[1] = jnp.exp(rate[...] * (-float(block_rows)))
+    decays[2] = jnp.exp(rate[...] * (-float(block_rows - 2)))
+    decays[3] = jnp.exp(rate[...])
 
     def arrived(k, slot, plane_now, origin):
         gather_copy(k, slot, plane_now, origin, partner).wait_recv()
@@ -188,23 +195,16 @@
 
     each_slice(project)
 
-    halo_copy = pltpu.make_async_remote_copy(
-        src_ref=proj.at[SEGMENTS - 1, pl.ds(seg - 8, 8), :], dst_ref=halo,
-        send_sem=halo_send, recv_sem=halo_recv,
-        device_id=at((ctx + 1) % n_ctx, plane, z), device_id_type=MESH,
-    )
-    halo_copy.start()
     taps32 = taps[...].astype(jnp.float32)
+
+    def tap(j, g):
+        return taps32[j, g : g + 1, :]
 
     def short_mix(i, now, one, two):
         featured = []
         for g in range(3):
             group = slice(g * channels, (g + 1) * channels)
-            featured.append(
-                taps32[0, g : g + 1, :] * now[:, group]
-                + taps32[1, g : g + 1, :] * one[:, group]
-                + taps32[2, g : g + 1, :] * two[:, group]
-            )
+            featured.append(tap(0, g) * now[:, group] + tap(1, g) * one[:, group] + tap(2, g) * two[:, group])
         sig[i] = featured[0] * featured[2]
         gate[i] = featured[1]
 
@@ -212,62 +212,99 @@
         short_mix(i, proj[:, i, :], proj[:, i - 1, :], proj[:, i - 2, :])
         return carry
 
-    lax.fori_loop(2, seg, short_step, 0)
+    lax.fori_loop(2, seg, short_step, 0, unroll=6)
+
+    first_row = lax.broadcasted_iota(jnp.int32, (SEGMENTS, 3 * channels), 0) == 0
+    first_sig = lax.broadcasted_iota(jnp.int32, (SEGMENTS, channels), 0) == 0
+    row_zero, row_next = proj[:, 0, :], proj[:, 1, :]
+    row_one = pltpu.roll(proj[:, seg - 1, :], 1, 0)
+    row_two = pltpu.roll(proj[:, seg - 2, :], 1, 0)
+    short_mix(0, row_zero, row_one, row_two)
+    short_mix(1, row_next, row_zero, row_one)
+    sig[0] = jnp.where(first_sig, 0.0, sig[0])
+    sig[1] = jnp.where(first_sig, 0.0, sig[1])
 
     halves = [pl.ds(first, 128) for first in range(0, channels, 128)]
+    lane = lax.broadcasted_iota(jnp.int32, (modes, SEGMENTS, 128), 1)
     for half in halves:
 
         def end_step(i, carry, half=half):
             return dec[:, :, half] * carry + sig[i, :, half][None]
 
-        ends[:, :, half] = lax.fori_loop(2, seg, end_step, jnp.zeros((modes, SEGMENTS, 128), jnp.float32))
-    far[...] = jnp.exp(step3[...] * (-float(seg - 2)))
-
-    halo_copy.wait_recv()
-    first_row = lax.broadcasted_iota(jnp.int32, (SEGMENTS, 3 * channels), 0) == 0
-    first_block = ctx == 0
-
-    def entering(row, last):
-        before = jnp.where(first_block, 0.0, halo[row : row + 1, :])
-        return jnp.where(first_row, jnp.broadcast_to(before, last.shape), pltpu.roll(last, 1, 0))
-
-    row_one = entering(7, proj[:, seg - 1, :])
-    row_two = entering(6, proj[:, seg - 2, :])
-    row_zero = proj[:, 0, :]
-    short_mix(0, row_zero, row_one, row_two)
-    short_mix(1, proj[:, 1, :], row_zero, row_one)
-
-    lane = lax.broadcasted_iota(jnp.int32, (modes, SEGMENTS, 128), 1)
-    for half in halves:
-        total = ends[:, :, half] + far[:, :, half] * (dec[:, :, half] * sig[0, :, half][None] + sig[1, :, half][None])
-        leap = far[:, :, half] * dec[:, :, half] * dec[:, :, half]
+        total = lax.fori_loop(0, seg, end_step, jnp.zeros((modes, SEGMENTS, 128), jnp.float32), unroll=8)
+        leap = far[:, :, half]
         for hop in (1, 2, 4):
-            moved = pltpu.roll(total, hop, 1)
-            total = total + jnp.where(lane >= hop, leap * moved, 0.0)
+            total = total + jnp.where(lane >= hop, leap * pltpu.roll(total, hop, 1), 0.0)
             leap = leap * leap
         ends[:, :, half] = total
-    state[...] = ends[:, SEGMENTS - 1, :].astype(jnp.bfloat16)
-    state_copies = [
+
+    message[0:modes, :] = ends[:, SEGMENTS - 1, :].astype(jnp.bfloat16)
+    last = [proj[SEGMENTS - 1, seg - 2 : seg - 1, :], proj[SEGMENTS - 1, seg - 1 : seg, :]]
+    outer = [row_zero[0:1, :], row_next[0:1, :]] + last
+    rows32[...] = jnp.zeros(rows32.shape, jnp.float32)
+    for r, row in enumerate(outer):
+        rows32[r : r + 1, :] = row[:, 0:channels]
+        rows32[4 + r : 5 + r, :] = row[:, 2 * channels :]
+    for r, row in enumerate(last):
+        rows32[8 + r : 9 + r, :] = row[:, channels : 2 * channels]
+    message[modes:, :] = rows32[...].astype(jnp.bfloat16)
+    copies = [
         pltpu.make_async_remote_copy(
-            src_ref=state, dst_ref=states.at[o - 1], send_sem=st_send.at[o - 1], recv_sem=st_recv.at[o - 1],
+            src_ref=message, dst_ref=messages.at[o - 1], send_sem=st_send.at[o - 1], recv_sem=st_recv.at[o - 1],
             device_id=at((ctx + o) % n_ctx, plane, z), device_id_type=MESH,
         )
         for o in range(1, n_ctx)
     ]
-    for copy in state_copies:
+    for copy in copies:
         copy.start()
-    segment = lax.broadcasted_iota(jnp.int32, (modes, SEGMENTS, channels), 1)
-    step3[...] = jnp.exp(step3[...] * (segment.astype(jnp.float32) * (-float(seg))))
+
     for half in halves:
         ends[:, :, half] = jnp.where(lane >= 1, pltpu.roll(ends[:, :, half], 1, 1), 0.0)
-    block_decay = jnp.exp(rate[...] * (-float(block_rows)))
+
+    def drain_gather(k):
+        for slot in range(SLOTS):
+            gather_copy(k, slot, plane, z, partner).wait_send()
+
+    each_slice(drain_gather)
+
+    for o in range(1, n_ctx):
+        copies[o - 1].wait_recv()
+        before[o - 1] = jnp.where(o <= ctx, messages[o - 1, modes:, :].astype(jnp.float32), 0.0)
+    before[n_ctx - 1] = jnp.zeros(before.shape[1:], jnp.float32)
+    before[n_ctx] = jnp.zeros(before.shape[1:], jnp.float32)
+
+    def first_two(r, g):
+        start, then = before[0:n_ctx, r, :], before[0:n_ctx, r + 1, :]
+        two, one = before[1 : n_ctx + 1, r + 2, :], before[1 : n_ctx + 1, r + 3, :]
+        return (
+            tap(0, g) * start + tap(1, g) * one + tap(2, g) * two,
+            tap(0, g) * then + tap(1, g) * start + tap(2, g) * one,
+        )
+
+    left, right = first_two(0, 0), first_two(4, 2)
+    heads[0] = left[0] * right[0]
+    heads[1] = left[1] * right[1]
+    decay = decays[0]
     incoming = jnp.zeros(rate.shape, jnp.float32)
     for o in range(n_ctx - 1, 0, -1):
-        state_copies[o - 1].wait_recv()
-        incoming = block_decay * incoming + jnp.where(o <= ctx, states[o - 1].astype(jnp.float32), 0.0)
-    inc[...] = incoming
+        ended = jnp.where(o <= ctx, messages[o - 1, 0:modes, :].astype(jnp.float32), 0.0)
+        head = decay * heads[0, o - 1 : o, :] + heads[1, o - 1 : o, :]
+        incoming = decays[1] * incoming + (ended + decays[2] * head)
+
+    def halo(r):
+        row = jnp.concatenate([before[0, r : r + 1, :], before[0, 8 + r - 2 : 9 + r - 2, :], before[0, 4 + r : 5 + r, :]], axis=1)
+        return jnp.broadcast_to(row, (SEGMENTS, 3 * channels))
+
+    row_one = jnp.where(first_row, halo(3), pltpu.roll(proj[:, seg - 1, :], 1, 0))
+    row_two = jnp.where(first_row, halo(2), pltpu.roll(proj[:, seg - 2, :], 1, 0))
+    row_zero = proj[:, 0, :]
+    short_mix(0, row_zero, row_one, row_two)
+    short_mix(1, proj[:, 1, :], row_zero, row_one)
+    inc[0] = incoming
+    inc[1] = incoming + decays[3] * (sig[0, 0:1, :] + decays[3] * sig[1, 0:1, :])
+    first_sig = lax.broadcasted_iota(jnp.int32, (SEGMENTS, channels), 0) == 0
     for m in range(modes):
-        ends[m] = ends[m] + step3[m] * inc[m : m + 1, :]
+        ends[m] = ends[m] + step3[m] * jnp.where(first_sig, inc[0, m : m + 1, :], inc[1, m : m + 1, :])
 
     for half in halves:
 
@@ -278,7 +315,7 @@
             gated32[i, :, half] = gate[i, :, half] * (mixed + skip[:, half] * now)
             return carry
 
-        lax.fori_loop(0, seg, long_step, ends[:, :, half])
+        lax.fori_loop(0, seg, long_step, ends[:, :, half], unroll=4)
     for s in range(SEGMENTS):
         gated[s * seg : (s + 1) * seg, :] = gated32[:, s, :].astype(jnp.bfloat16)
 
@@ -340,26 +377,26 @@
     for body in (reduce_one, reduce_two, reduce_three, reduce_four):
         each_slice(body)
 
+    late = (CROSS, OWN[0, 1], OWN[1, 1])
+
+    def drain_scatter(k):
+        for slot in range(SLOTS):
+            if slot not in late:
+                scatter_copy(k, slot, plane, z, partner).wait_send()
+
+    each_slice(drain_scatter)
     for k in range(SLICES):
-        total = part[k, block(plane, z), :].astype(jnp.float32)
-        for slot in (CROSS, OWN[0, 1], OWN[1, 1]):
+        columns = pl.ds(k * cols, cols)
+        total = part[k, block(plane, z), :].astype(jnp.float32) + tok[:, columns].astype(jnp.float32)
+        for slot in late:
             scatter_copy(k, slot, plane, z, partner).wait_recv()
             total = total + land[k, slot].astype(jnp.float32)
-        total = total + tok[:, k * cols : (k + 1) * cols].astype(jnp.float32)
-        outv[:, k * cols : (k + 1) * cols] = total.astype(jnp.bfloat16)
-    write = pltpu.make_async_copy(outv, out_hbm, out_sem)
-    write.start()
-
-    def drain(k):
-        for slot in range(SLOTS):
-            gather_copy(k, slot, plane, z, partner).wait_send()
+        out[:, columns] = total.astype(jnp.bfloat16)
+    for k in range(SLICES):
+        for slot in late:
             scatter_copy(k, slot, plane, z, partner).wait_send()
-
-    each_slice(drain)
-    halo_copy.wait_send()
-    for copy in state_copies:
+    for copy in copies:
         copy.wait_send()
-    write.wait()
 
 
 def on_device(ring, n_ctx, tokens, norm_gain, in_weight, short_filter, residues, decay_rate, skip_gain, out_weight):
@@ -374,9 +411,9 @@
     dma = pltpu.SemaphoreType.DMA
     return pl.pallas_call(
         functools.partial(kernel, (ring, n_ctx, rows, width)),
-        out_shape=jax.ShapeDtypeStruct((rows, width), bf16),
+        out_shape=pltpu.VMEM((rows, width), bf16),
         in_specs=[any_spec] * 8,
-        out_specs=any_spec,
+        out_specs=pl.BlockSpec(memory_space=pltpu.VMEM),
         scratch_shapes=[
             pltpu.VMEM((rows, width), bf16),
             pltpu.VMEM((1, width), f32),
@@ -388,31 +425,31 @@
             pltpu.VMEM((channels, width), bf16),
             pltpu.VMEM((SLICES, block_rows, cols), bf16),
             pltpu.VMEM((SEGMENTS, seg, 3 * channels), f32),
-            pltpu.VMEM((8, 3 * channels), f32),
             pltpu.VMEM((seg, SEGMENTS, channels), f32),
             pltpu.VMEM((seg, SEGMENTS, channels), f32),
             table, table, table, table, table,
-            pltpu.VMEM((modes, channels), bf16),
-            pltpu.VMEM((n_ctx - 1, modes, channels), bf16),
-            pltpu.VMEM((modes, channels), f32),
+            pltpu.VMEM((modes + 16, channels), bf16),
+            pltpu.VMEM((n_ctx - 1, modes + 16, channels), bf16),
+            pltpu.VMEM((16, channels), f32),
+            pltpu.VMEM((n_ctx + 1, 16, channels), f32),
+            pltpu.VMEM((2, n_ctx, channels), f32),
+            pltpu.VMEM((4, modes, channels), f32),
+            pltpu.VMEM((2, modes, channels), f32),
             pltpu.VMEM((seg, SEGMENTS, channels), f32),
             pltpu.VMEM((block_rows, channels), bf16),
             pltpu.VMEM((SLICES, block_rows, cols), bf16),
             pltpu.VMEM((SLICES, SLOTS, rows, cols), bf16),
-            pltpu.VMEM((rows, width), bf16),
             dma((8,)),
             dma((SLICES, SLOTS)), dma((SLICES, SLOTS)),
             dma((SLICES, SLOTS)), dma((SLICES, SLOTS)),
-            dma, dma,
             dma((n_ctx - 1,)), dma((n_ctx - 1,)),
-            dma,
         ],
         name="hyena_layer",
         cost_estimate=pl.CostEstimate(
             flops=2 * block_rows * width * channels * 4, bytes_accessed=8 * width * channels, transcendentals=0
         ),
         compiler_params=pltpu.CompilerParams(
-            collective_id=0, has_side_effects=True, vmem_limit_bytes=64 * 2**20
+            collective_id=0, has_side_effects=True, vmem_limit_bytes=60 * 2**20
         ),
     )(
         tokens, norm_gain.reshape(1, width), in_weight.transpose(1, 0, 2), short_filter,

time: 63.3 us -> 59.9 us (0.946)
  Pallas kernels: 61.6 us -> 59 us
  local copies, waits for them, and re-layouts: 1.57 us -> 0.66 us
    pallas_call x1, Pallas kernels: 61.6 us -> 59 us  [on_device(): pl.pallas_call(functools.partial(kernel, (ring, n_ctx, rows, width)), out...]
    unnamed x1, local copies, waits for them, and re-layouts: 1.57 us -> 0.66 us
where the time goes in v3:
time: 59.9 us; the launch traced here: 59.6 us
  Pallas kernels  59 us (98%)
  local copies, waits for them, and re-layouts  0.66 us (1%)
    pallas_call x1, Pallas kernels, on_device(): pl.pallas_call(functools.partial(kernel, (ring, n_ctx, rows, width)), out...  59 us

profile of v3, /device:TPU:2, one launch (start us, length us, event | category | flops | bytes accessed | tf_op | source)
XLA Modules:
  0.0 59.6 jit_solution(3726983634198654476)
XLA Ops:
  0.0 59.0 %hyena_layer.1 = bf16[16,4096]{1,0:T(8,128)(2,1)S(1)} custom-call(bf16[16,4096]{1,0:T(8,128)(2,1)} %tokens_hbm.1, f32[1,4096]{1,0:T(1,128)} %bitcast.4, bf16[3,4096,256]{2,1,0:T(8,128)(2,1)} %bitcast.3, bf16[3,3,256]{2,1,0:T(4,128)(2,1)} %taps_hbm.1, f32[16,256]{1,0:T(8,128)} %res_hbm.1, f32[16,256]{1,0:T(8,128)} %rate_hbm.1, f32[1,256]{1,0:T(1,128)} %bitcast.5, ...), custom_call_target="tpu_custom_call" | custom-call | flops 2147483648 | bytes 8388608 | tf_op jit(solution)/shard_map/hyena_layer/pallas_call | solution.py:412
  59.0 0.7 %copy.10 = bf16[16,4096]{1,0:T(8,128)(2,1)} copy(bf16[16,4096]{1,0:T(8,128)(2,1)S(1)} %hyena_layer.1) | data formatting | bytes 262144

commit v4 on v3

--- a/solution.py
+++ b/solution.py
@@ -11,11 +11,44 @@
 MESH = pl.DeviceIdType.MESH
 SLICES = 4
 SEGMENTS = 8
-OWN = {(0, j): j - 1 for j in (1, 2, 3, 4)} | {(1, j): 3 + j for j in (1, 2, 3)}
-OTH = {(0, j): 7 + j for j in (1, 2, 3, 4)} | {(1, j): 11 + j for j in (1, 2, 3)}
-CROSS = 7
+STEPS = (1, 2, 3, 4, -1, -2, -3)
+GATHER_FROM = (
+    {-3: -2, -2: -1, -1: 0, 0: "x", 1: "x", 2: 1, 3: "x", 4: 3},
+    {-3: -2, -2: -1, -1: "x", 0: "x", 1: 0, 2: "x", 3: "x", 4: "x"},
+    {-3: -2, -2: "x", -1: "x", 0: "x", 1: "x", 2: 1, 3: "x", 4: "x"},
+    {-3: -2, -2: "x", -1: "x", 0: "x", 1: "x", 2: 1, 3: "x", 4: 3},
+)
+SCATTER_TO = (
+    {-3: "x", -2: "x", -1: -2, 0: "x", 1: 0, 2: "x", 3: 2, 4: 3},
+    {-3: -2, -2: "x", -1: "x", 0: "x", 1: "x", 2: 1, 3: "x", 4: "x"},
+    {-3: -2, -2: -1, -1: "x", 0: "x", 1: "x", 2: 3, 3: "x", 4: 3},
+    {-3: "x", -2: "x", -1: 0, 0: "x", 1: 0, 2: 1, 3: "x", 4: "x"},
+)
+GATHER_ORDER = (
+    (0, "o", 1), (1, "o", 1), (3, "o", 1), (0, "t", 0), (2, "o", 1), (2, "o", -1), (1, "o", -1), (1, "t", 0),
+    (2, "t", 0), (0, "o", -1), (3, "o", -1), (0, "t", 1), (0, "o", 2), (1, "o", 2), (3, "o", 2), (2, "o", 2),
+    (3, "t", 1), (2, "t", 1), (2, "t", -1), (2, "o", -2), (1, "o", -2), (0, "t", -1), (0, "o", 3),
+    (1, "t", -1), (3, "t", -1), (1, "o", 3), (3, "o", -2), (2, "o", 3), (3, "o", 3), (0, "o", -2),
+    (0, "o", 4), (0, "t", 3), (2, "t", -2), (2, "o", -3), (0, "t", -2), (0, "t", 2), (1, "t", 3),
+    (2, "o", 4), (1, "o", 4), (3, "t", 3), (2, "t", 3), (1, "o", -3), (3, "t", -2), (1, "t", -2),
+    (0, "o", -3), (0, "t", -3), (2, "t", 4), (0, "t", 4), (1, "t", 2), (2, "t", -3), (2, "t", 2),
+    (1, "t", 4), (3, "o", -3), (3, "o", 4), (3, "t", 0), (1, "t", 1), (3, "t", 4), (1, "t", -3),
+    (3, "t", -3), (3, "t", 2), (0, "P", 0), (2, "P", 0), (1, "P", 0), (3, "P", 0),
+)
+SCATTER_ORDER = (
+    (1, "M", 0), (1, "t", -3), (1, "t", 4), (2, "M", 0), (2, "t", 2), (1, "t", 3), (2, "t", 4), (2, "o", 4),
+    (3, "M", 0), (3, "t", 4), (2, "t", -3), (0, "M", 0), (0, "t", 4), (3, "t", 2), (1, "o", -3),
+    (0, "t", -1), (0, "t", -3), (3, "t", -3), (2, "o", -3), (0, "o", 4), (1, "o", 4), (2, "t", 3),
+    (2, "t", -2), (3, "t", 3), (3, "o", 4), (0, "t", 3), (3, "t", -2), (0, "o", -3), (1, "t", 2),
+    (3, "t", -1), (1, "t", -2), (0, "t", -2), (1, "o", 3), (2, "o", 3), (3, "o", -3), (0, "o", 3),
+    (3, "o", 3), (0, "t", 2), (1, "t", -1), (3, "t", 1), (2, "t", 1), (1, "o", -2), (0, "t", 1), (1, "t", 1),
+    (2, "t", -1), (1, "o", 2), (2, "o", 2), (2, "o", -2), (3, "o", 2), (3, "o", -2), (1, "t", 0),
+    (2, "t", 0), (0, "o", -2), (0, "o", 2), (1, "o", 1), (1, "o", -1), (3, "t", 0), (2, "o", 1),
+    (2, "o", -1), (0, "t", 0), (3, "o", 1), (3, "o", -1), (0, "o", -1), (0, "o", 1), (1, "F", 0),
+    (2, "F", 0), (3, "F", 0), (0, "F", 0),
+)
+SLOT = {("o", p): i for i, p in enumerate(STEPS)} | {("t", p): 7 + i for i, p in enumerate((0,) + STEPS)}
 SLOTS = 15
-REACH = (4, 3)
 
 
 def kernel(
@@ -59,33 +92,33 @@
     for peer in peers:
         pl.semaphore_signal(barrier, inc=1, device_id=peer, device_id_type=MESH)
 
-    def ring_at(k, chain, steps):
-        sign = 1 - 2 * (k % 2) if chain == 0 else 2 * (k % 2) - 1
-        return (z + sign * steps + 2 * ring) % ring
+    def ring_at(k, steps):
+        return (z + (1 - 2 * (k % 2)) * steps + 2 * ring) % ring
+
+    def where(kind, k, position):
+        return (plane if kind == "o" else 1 - plane), ring_at(k, -position)
 
     def block(plane_now, z_now):
         return pl.ds(pl.multiple_of((plane_now * ring + z_now) * rows, rows), rows)
 
-    def gather_copy(k, slot, plane_now, z_now, target):
-        where = xg.at[k, block(plane_now, z_now), :]
+    def gather_copy(k, kind, position, source_kind, source, target):
+        mine = xg.at[k, block(*where(source_kind, k, source)), :]
+        slot = SLOT[kind, position]
         return pltpu.make_async_remote_copy(
-            src_ref=where, dst_ref=where, send_sem=ag_send.at[k, slot], recv_sem=ag_recv.at[k, slot],
+            src_ref=mine, dst_ref=mine, send_sem=ag_send.at[k, slot], recv_sem=ag_recv.at[k, slot],
             device_id=target, device_id_type=MESH,
         )
 
-    def scatter_copy(k, slot, plane_now, z_now, target):
+    def scatter_copy(k, kind, position, target):
+        slot = SLOT[kind, position]
         return pltpu.make_async_remote_copy(
-            src_ref=part.at[k, block(plane_now, z_now), :], dst_ref=land.at[k, slot],
+            src_ref=part.at[k, block(*where(kind, k, position)), :], dst_ref=land.at[k, slot],
             send_sem=rs_send.at[k, slot], recv_sem=rs_recv.at[k, slot],
             device_id=target, device_id_type=MESH,
         )
 
-    def each_slice(body):
-        def step(k, carry):
-            body(k)
-            return carry
-
-        lax.fori_loop(0, SLICES, step, 0, unroll=True)
+    def toward(position):
+        return position - 1 if position > 0 else position + 1
 
     loads[0].wait()
     loads[1].wait()
@@ -96,12 +129,31 @@
         xg[k, block(plane, z), :] = normed[:, k * cols : (k + 1) * cols]
     pl.semaphore_wait(barrier, len(peers))
 
-    def start_own(k):
-        gather_copy(k, OWN[0, 1], plane, z, at(ctx, plane, ring_at(k, 0, 1))).start()
-        gather_copy(k, OWN[1, 1], plane, z, at(ctx, plane, ring_at(k, 1, 1))).start()
-        gather_copy(k, CROSS, plane, z, partner).start()
-
-    each_slice(start_own)
+    got = set()
+
+    def need(k, kind, position):
+        if (k, kind, position) not in got:
+            got.add((k, kind, position))
+            gather_copy(k, kind, position, kind, position, partner).wait_recv()
+
+    def send_gather(k, kind, position):
+        if kind == "o":
+            source = toward(position)
+            if source:
+                need(k, "o", source)
+            gather_copy(k, "o", position, "o", source, at(ctx, plane, ring_at(k, position - source))).start()
+        elif GATHER_FROM[k][position] == "x":
+            if position:
+                need(k, "o", position)
+            gather_copy(k, "t", position, "o", position, partner).start()
+        else:
+            source = GATHER_FROM[k][position]
+            need(k, "t", source)
+            gather_copy(k, "t", position, "t", source, at(ctx, plane, ring_at(k, position - source))).start()
+
+    first_wait = next(i for i, (k, kind, p) in enumerate(GATHER_ORDER) if (kind, p) not in (("o", 1), ("o", -1), ("t", 0)))
+    for step in GATHER_ORDER[:first_wait]:
+        send_gather(*step)
 
     loads[2].wait()
     loads[3].wait()
@@ -120,80 +172,29 @@
     decays[2] = jnp.exp(rate[...] * (-float(block_rows - 2)))
     decays[3] = jnp.exp(rate[...])
 
-    def arrived(k, slot, plane_now, origin):
-        gather_copy(k, slot, plane_now, origin, partner).wait_recv()
-
-    def along(k, chain, table, j, plane_now):
-        target = at(ctx, plane, ring_at(k, chain, 1))
-        gather_copy(k, table[chain, j], plane_now, ring_at(k, chain, 1 - j), target).start()
-
-    def across(k, chain, j):
-        gather_copy(k, OTH[chain, j], plane, ring_at(k, chain, -j), partner).start()
-
-    def got_own(k, chain, j):
-        arrived(k, OWN[chain, j], plane, ring_at(k, chain, -j))
-
-    def got_other(k, chain, j):
-        arrived(k, OTH[chain, j], 1 - plane, ring_at(k, chain, -j))
-
-    def gather_one(k):
-        got_own(k, 0, 1)
-        along(k, 0, OWN, 2, plane)
-        across(k, 0, 1)
-        got_own(k, 1, 1)
-        along(k, 1, OWN, 2, plane)
-
-    def gather_two(k):
-        got_own(k, 0, 2)
-        along(k, 0, OWN, 3, plane)
-        got_own(k, 1, 2)
-        along(k, 1, OWN, 3, plane)
-        across(k, 1, 2)
-
-    def gather_three(k):
-        got_own(k, 0, 3)
-        along(k, 0, OWN, 4, plane)
-        across(k, 0, 3)
-        arrived(k, CROSS, 1 - plane, z)
-        along(k, 1, OTH, 1, 1 - plane)
-        got_own(k, 1, 3)
-        across(k, 1, 3)
-
-    def gather_four(k):
-        got_other(k, 0, 1)
-        along(k, 0, OTH, 2, 1 - plane)
-
-    def gather_five(k):
-        got_other(k, 0, 3)
-        along(k, 0, OTH, 4, 1 - plane)
-
-    for body in (gather_one, gather_two, gather_three, gather_four, gather_five):
-        each_slice(body)
-
-    loads[6].wait()
-
     def project(k):
-        got_own(k, 0, 4)
-        got_other(k, 1, 1)
-        got_other(k, 1, 2)
-        got_other(k, 0, 2)
-        got_other(k, 1, 3)
-        got_other(k, 0, 4)
-        depth = pl.ds(pl.multiple_of(k * cols, cols), cols)
+        for p in STEPS:
+            need(k, "o", p)
+        for p in (0,) + STEPS:
+            need(k, "t", p)
         for g in range(3):
             group = pl.ds(g * channels, channels)
-            product = jnp.dot(xg[k], win[g, depth, :], preferred_element_type=jnp.float32)
+            product = jnp.dot(xg[k], win[g, k * cols : (k + 1) * cols, :], preferred_element_type=jnp.float32)
             product = product.reshape(SEGMENTS, seg, channels)
-
-            @pl.when(k == 0)
-            def _():
+            if len(projected) == 0:
                 proj[:, :, group] = product
-
-            @pl.when(k > 0)
-            def _():
+            else:
                 proj[:, :, group] += product
-
-    each_slice(project)
+        projected.append(k)
+
+    projected = []
+    for k, kind, position in GATHER_ORDER[first_wait:]:
+        if kind == "P":
+            if not projected:
+                loads[6].wait()
+            project(k)
+        else:
+            send_gather(k, kind, position)
 
     taps32 = taps[...].astype(jnp.float32)
 
@@ -261,11 +262,9 @@
     for half in halves:
         ends[:, :, half] = jnp.where(lane >= 1, pltpu.roll(ends[:, :, half], 1, 1), 0.0)
 
-    def drain_gather(k):
-        for slot in range(SLOTS):
-            gather_copy(k, slot, plane, z, partner).wait_send()
-
-    each_slice(drain_gather)
+    for k in range(SLICES):
+        for kind, position in SLOT:
+            gather_copy(k, kind, position, kind, position, partner).wait_send()
 
     for o in range(1, n_ctx):
         copies[o - 1].wait_recv()
@@ -321,80 +320,51 @@
 
     loads[7].wait()
 
-    def send_along(k, chain, j, plane_now, table):
-        target = at(ctx, plane, ring_at(k, chain, -1))
-        scatter_copy(k, table[chain, j], plane_now, ring_at(k, chain, -j), target).start()
-
-    def send_across(k, chain, j):
-        scatter_copy(k, OTH[chain, j], 1 - plane, ring_at(k, chain, -j), partner).start()
-
-    def add(k, plane_now, z_now, slots):
-        where = block(plane_now, z_now)
-        total = part[k, where, :].astype(jnp.float32)
-        for slot in slots:
-            scatter_copy(k, slot, plane_now, z_now, partner).wait_recv()
-            total = total + land[k, slot].astype(jnp.float32)
-        part[k, where, :] = total.astype(jnp.bfloat16)
-
-    def multiply(k):
-        depth = pl.ds(pl.multiple_of(k * cols, cols), cols)
-        part[k] = jnp.dot(gated[...], wout[:, depth], preferred_element_type=jnp.float32).astype(jnp.bfloat16)
-        send_across(k, 1, 3)
-        send_along(k, 0, 4, 1 - plane, OTH)
-        send_along(k, 0, 4, plane, OWN)
-        send_along(k, 1, 1, 1 - plane, OTH)
-        send_along(k, 0, 2, 1 - plane, OTH)
-
-    each_slice(multiply)
-
-    def reduce_one(k):
-        add(k, 1 - plane, ring_at(k, 0, -3), [OTH[0, 4]])
-        send_across(k, 0, 3)
-        add(k, plane, ring_at(k, 1, -3), [OTH[1, 3]])
-        send_along(k, 1, 3, plane, OWN)
-        send_across(k, 1, 2)
-
-    def reduce_two(k):
-        add(k, plane, ring_at(k, 0, -3), [OWN[0, 4], OTH[0, 3]])
-        send_along(k, 0, 3, plane, OWN)
-        add(k, 1 - plane, ring_at(k, 0, -1), [OTH[0, 2]])
-        send_across(k, 0, 1)
-
-    def reduce_three(k):
-        add(k, plane, ring_at(k, 1, -2), [OWN[1, 3], OTH[1, 2]])
-        send_along(k, 1, 2, plane, OWN)
-        add(k, plane, ring_at(k, 0, -2), [OWN[0, 3]])
-        send_along(k, 0, 2, plane, OWN)
-        add(k, 1 - plane, z, [OTH[1, 1]])
-        scatter_copy(k, CROSS, 1 - plane, z, partner).start()
-
-    def reduce_four(k):
-        add(k, plane, ring_at(k, 1, -1), [OWN[1, 2]])
-        send_along(k, 1, 1, plane, OWN)
-        add(k, plane, ring_at(k, 0, -1), [OTH[0, 1], OWN[0, 2]])
-        send_along(k, 0, 1, plane, OWN)
-
-    for body in (reduce_one, reduce_two, reduce_three, reduce_four):
-        each_slice(body)
-
-    late = (CROSS, OWN[0, 1], OWN[1, 1])
-
-    def drain_scatter(k):
-        for slot in range(SLOTS):
-            if slot not in late:
-                scatter_copy(k, slot, plane, z, partner).wait_send()
-
-    each_slice(drain_scatter)
+    def add(k, kind, position, terms):
+        for term in terms:
+            scatter_copy(k, *term, partner).wait_recv()
+        mine = block(*where(kind, k, position))
+        total = part[k, mine, :].astype(jnp.float32)
+        for term in terms:
+            total = total + land[k, SLOT[term]].astype(jnp.float32)
+        return mine, total
+
+    def terms_of(k, kind, position):
+        terms = [("t", p) for p in STEPS if kind == "t" and SCATTER_TO[k][p] == position]
+        if kind == "o":
+            terms += [("o", p) for p in STEPS if toward(p) == position]
+            terms += [("t", position)] if SCATTER_TO[k][position] == "x" else []
+        return terms
+
+    def send_scatter(k, kind, position):
+        terms = terms_of(k, kind, position)
+        if terms:
+            mine, total = add(k, kind, position, terms)
+            part[k, mine, :] = total.astype(jnp.bfloat16)
+        target = toward(position) if kind == "o" else SCATTER_TO[k][position]
+        device = partner if target == "x" else at(ctx, plane, ring_at(k, target - position))
+        scatter_copy(k, kind, position, device).start()
+
+    late = (("t", 0), ("o", 1), ("o", -1))
+
+    def drain(k, kinds):
+        for kind, position in kinds:
+            scatter_copy(k, kind, position, partner).wait_send()
+
+    finished = []
+    for k, kind, position in SCATTER_ORDER:
+        columns = slice(k * cols, (k + 1) * cols)
+        if kind == "M":
+            product = jnp.dot(gated[...], wout[:, columns], preferred_element_type=jnp.float32)
+            part[k] = product.astype(jnp.bfloat16)
+        elif kind == "F":
+            drain(k, [other for other in SLOT if other not in late])
+            _, total = add(k, "o", 0, terms_of(k, "o", 0))
+            out[:, columns] = (total + tok[:, columns].astype(jnp.float32)).astype(jnp.bfloat16)
+        else:
+            send_scatter(k, kind, position)
     for k in range(SLICES):
-        columns = pl.ds(k * cols, cols)
-        total = part[k, block(plane, z), :].astype(jnp.float32) + tok[:, columns].astype(jnp.float32)
-        for slot in late:
-            scatter_copy(k, slot, plane, z, partner).wait_recv()
-            total = total + land[k, slot].astype(jnp.float32)
-        out[:, columns] = total.astype(jnp.bfloat16)
-    for k in range(SLICES):
-        for slot in late:
-            scatter_copy(k, slot, plane, z, partner).wait_send()
+        drain(k, late)
     for copy in copies:
         copy.wait_send()
 

time: 59.9 us -> 58.8 us (0.982)
  Pallas kernels: 59 us -> 57.5 us
    pallas_call x1, Pallas kernels: 59 us -> 57.5 us  [on_device(): pl.pallas_call(functools.partial(kernel, (ring, n_ctx, rows, width)), out...]
where the time goes in v4:
time: 58.8 us; the launch traced here: 58.2 us
  Pallas kernels  57.5 us (98%)
  local copies, waits for them, and re-layouts  0.66 us (1%)
    pallas_call x1, Pallas kernels, on_device(): pl.pallas_call(functools.partial(kernel, (ring, n_ctx, rows, width)), out...  57.5 us

profile of v4, /device:TPU:2, one launch (start us, length us, event | category | flops | bytes accessed | tf_op | source)
XLA Modules:
  0.0 58.2 jit_solution(15098378995157192259)
XLA Ops:
  0.0 57.5 %hyena_layer.1 = bf16[16,4096]{1,0:T(8,128)(2,1)S(1)} custom-call(bf16[16,4096]{1,0:T(8,128)(2,1)} %tokens_hbm.1, f32[1,4096]{1,0:T(1,128)} %bitcast.4, bf16[3,4096,256]{2,1,0:T(8,128)(2,1)} %bitcast.3, bf16[3,3,256]{2,1,0:T(4,128)(2,1)} %taps_hbm.1, f32[16,256]{1,0:T(8,128)} %res_hbm.1, f32[16,256]{1,0:T(8,128)} %rate_hbm.1, f32[1,256]{1,0:T(1,128)} %bitcast.5, ...), custom_call_target="tpu_custom_call" | custom-call | flops 2147483648 | bytes 8388608 | tf_op jit(solution)/shard_map/hyena_layer/pallas_call | solution.py:382
  57.5 0.7 %copy.10 = bf16[16,4096]{1,0:T(8,128)(2,1)} copy(bf16[16,4096]{1,0:T(8,128)(2,1)S(1)} %hyena_layer.1) | data formatting | bytes 262144

commit v5 on v4

--- a/solution.py
+++ b/solution.py
@@ -13,39 +13,51 @@
 SEGMENTS = 8
 STEPS = (1, 2, 3, 4, -1, -2, -3)
 GATHER_FROM = (
-    {-3: -2, -2: -1, -1: 0, 0: "x", 1: "x", 2: 1, 3: "x", 4: 3},
+    {-3: -2, -2: "x", -1: 0, 0: "x", 1: 2, 2: "x", 3: "x", 4: 3},
+    {-3: -2, -2: -1, -1: 0, 0: "x", 1: "x", 2: "x", 3: "x", 4: "x"},
+    {-3: "x", -2: "x", -1: 0, 0: "x", 1: 0, 2: 3, 3: "x", 4: 3},
+    {-3: "x", -2: "x", -1: "x", 0: "x", 1: 2, 2: "x", 3: "x", 4: 3},
+)
+SCATTER_TO = (
+    {-3: -2, -2: -1, -1: "x", 0: "x", 1: "x", 2: 1, 3: "x", 4: 3},
+    {-3: "x", -2: -1, -1: "x", 0: "x", 1: 0, 2: "x", 3: "x", 4: "x"},
+    {-3: -2, -2: "x", -1: "x", 0: "x", 1: "x", 2: "x", 3: "x", 4: 3},
     {-3: -2, -2: -1, -1: "x", 0: "x", 1: 0, 2: "x", 3: "x", 4: "x"},
-    {-3: -2, -2: "x", -1: "x", 0: "x", 1: "x", 2: 1, 3: "x", 4: "x"},
-    {-3: -2, -2: "x", -1: "x", 0: "x", 1: "x", 2: 1, 3: "x", 4: 3},
-)
-SCATTER_TO = (
-    {-3: "x", -2: "x", -1: -2, 0: "x", 1: 0, 2: "x", 3: 2, 4: 3},
-    {-3: -2, -2: "x", -1: "x", 0: "x", 1: "x", 2: 1, 3: "x", 4: "x"},
-    {-3: -2, -2: -1, -1: "x", 0: "x", 1: "x", 2: 3, 3: "x", 4: 3},
-    {-3: "x", -2: "x", -1: 0, 0: "x", 1: 0, 2: 1, 3: "x", 4: "x"},
+)
+GATHER_OWN = (
+    {1: 0, 2: 0, 3: 2, 4: 3, -1: 0, -2: 0, -3: -2},
+    {1: 0, 2: 1, 3: 2, 4: 2, -1: 0, -2: -1, -3: -2},
+    {1: 0, 2: 0, 3: 2, 4: 3, -1: 0, -2: -1, -3: -2},
+    {1: 0, 2: 0, 3: 2, 4: 3, -1: 0, -2: -1, -3: -2},
+)
+SCATTER_OWN = (
+    {1: 0, 2: 1, 3: 1, 4: 3, -1: 0, -2: -1, -3: -2},
+    {1: 0, 2: 0, 3: 2, 4: 3, -1: 0, -2: -1, -3: -2},
+    {1: 0, 2: 0, 3: 2, 4: 3, -1: 0, -2: 0, -3: -2},
+    {1: 0, 2: 0, 3: 2, 4: 3, -1: 0, -2: -1, -3: -2},
 )
 GATHER_ORDER = (
-    (0, "o", 1), (1, "o", 1), (3, "o", 1), (0, "t", 0), (2, "o", 1), (2, "o", -1), (1, "o", -1), (1, "t", 0),
-    (2, "t", 0), (0, "o", -1), (3, "o", -1), (0, "t", 1), (0, "o", 2), (1, "o", 2), (3, "o", 2), (2, "o", 2),
-    (3, "t", 1), (2, "t", 1), (2, "t", -1), (2, "o", -2), (1, "o", -2), (0, "t", -1), (0, "o", 3),
-    (1, "t", -1), (3, "t", -1), (1, "o", 3), (3, "o", -2), (2, "o", 3), (3, "o", 3), (0, "o", -2),
-    (0, "o", 4), (0, "t", 3), (2, "t", -2), (2, "o", -3), (0, "t", -2), (0, "t", 2), (1, "t", 3),
-    (2, "o", 4), (1, "o", 4), (3, "t", 3), (2, "t", 3), (1, "o", -3), (3, "t", -2), (1, "t", -2),
-    (0, "o", -3), (0, "t", -3), (2, "t", 4), (0, "t", 4), (1, "t", 2), (2, "t", -3), (2, "t", 2),
-    (1, "t", 4), (3, "o", -3), (3, "o", 4), (3, "t", 0), (1, "t", 1), (3, "t", 4), (1, "t", -3),
-    (3, "t", -3), (3, "t", 2), (0, "P", 0), (2, "P", 0), (1, "P", 0), (3, "P", 0),
+    (3, "o", -1), (3, "o", 2), (2, "o", 2), (2, "t", 0), (0, "o", 2), (1, "t", 0), (1, "o", -1), (1, "o", 1),
+    (3, "t", 0), (2, "o", -1), (0, "o", -2), (3, "t", -1), (3, "t", 2), (0, "t", 0), (3, "o", -2),
+    (3, "o", 3), (1, "t", 1), (2, "o", 3), (1, "t", -1), (1, "o", 2), (2, "o", -2), (0, "o", 3), (3, "o", 1),
+    (0, "t", 2), (3, "o", -3), (2, "t", 1), (2, "t", -1), (0, "t", -2), (1, "o", -2), (3, "t", 3),
+    (1, "o", 4), (1, "t", 2), (2, "o", -3), (1, "o", 3), (0, "o", 1), (1, "t", -2), (2, "t", 3), (0, "t", 3),
+    (1, "o", -3), (3, "t", -2), (3, "t", -3), (3, "t", 4), (1, "t", 4), (3, "t", 1), (3, "o", 4),
+    (1, "t", -3), (2, "t", 2), (0, "o", -1), (0, "t", -1), (0, "o", -3), (1, "t", 3), (2, "t", -2),
+    (2, "o", 1), (2, "t", -3), (2, "o", 4), (2, "t", 4), (0, "t", 1), (0, "o", 4), (0, "t", 4), (0, "t", -3),
+    (3, "P", 0), (1, "P", 0), (2, "P", 0), (0, "P", 0),
 )
 SCATTER_ORDER = (
-    (1, "M", 0), (1, "t", -3), (1, "t", 4), (2, "M", 0), (2, "t", 2), (1, "t", 3), (2, "t", 4), (2, "o", 4),
-    (3, "M", 0), (3, "t", 4), (2, "t", -3), (0, "M", 0), (0, "t", 4), (3, "t", 2), (1, "o", -3),
-    (0, "t", -1), (0, "t", -3), (3, "t", -3), (2, "o", -3), (0, "o", 4), (1, "o", 4), (2, "t", 3),
-    (2, "t", -2), (3, "t", 3), (3, "o", 4), (0, "t", 3), (3, "t", -2), (0, "o", -3), (1, "t", 2),
-    (3, "t", -1), (1, "t", -2), (0, "t", -2), (1, "o", 3), (2, "o", 3), (3, "o", -3), (0, "o", 3),
-    (3, "o", 3), (0, "t", 2), (1, "t", -1), (3, "t", 1), (2, "t", 1), (1, "o", -2), (0, "t", 1), (1, "t", 1),
-    (2, "t", -1), (1, "o", 2), (2, "o", 2), (2, "o", -2), (3, "o", 2), (3, "o", -2), (1, "t", 0),
-    (2, "t", 0), (0, "o", -2), (0, "o", 2), (1, "o", 1), (1, "o", -1), (3, "t", 0), (2, "o", 1),
-    (2, "o", -1), (0, "t", 0), (3, "o", 1), (3, "o", -1), (0, "o", -1), (0, "o", 1), (1, "F", 0),
-    (2, "F", 0), (3, "F", 0), (0, "F", 0),
+    (2, "M", 0), (2, "t", -1), (2, "o", 4), (2, "t", 4), (2, "t", -3), (1, "M", 0), (1, "t", 4), (3, "M", 0),
+    (3, "o", 1), (3, "t", 4), (2, "o", -3), (2, "t", 2), (3, "t", -3), (0, "M", 0), (1, "t", -3),
+    (1, "t", -2), (0, "t", -3), (1, "t", 3), (3, "t", 3), (0, "t", 4), (0, "o", -3), (2, "o", -1),
+    (3, "o", -3), (3, "t", -2), (1, "o", 4), (2, "t", 3), (3, "o", 4), (0, "o", 4), (0, "t", 3),
+    (0, "t", -2), (0, "t", 2), (3, "t", 2), (3, "t", 1), (0, "o", -2), (1, "t", 2), (1, "o", -3),
+    (3, "o", -2), (1, "o", 3), (0, "o", 2), (2, "t", 1), (3, "o", 3), (3, "t", -1), (1, "t", 1),
+    (1, "t", -1), (2, "o", 3), (1, "o", 1), (2, "t", -2), (0, "t", 1), (1, "o", -2), (0, "o", 3),
+    (0, "t", -1), (1, "o", 2), (3, "o", 2), (2, "o", 2), (3, "t", 0), (1, "t", 0), (3, "o", -1), (2, "t", 0),
+    (0, "t", 0), (2, "o", 1), (2, "o", -2), (1, "o", -1), (0, "o", 1), (0, "o", -1), (1, "F", 0),
+    (3, "F", 0), (2, "F", 0), (0, "F", 0),
 )
 SLOT = {("o", p): i for i, p in enumerate(STEPS)} | {("t", p): 7 + i for i, p in enumerate((0,) + STEPS)}
 SLOTS = 15
@@ -87,7 +99,7 @@
         load.start()
 
     barrier = pltpu.get_barrier_semaphore()
-    peers = [partner, at(ctx, plane, (z + 1) % ring), at(ctx, plane, (z + ring - 1) % ring)]
+    peers = [partner] + [at(ctx, plane, (z + steps) % ring) for steps in (1, 2, ring - 2, ring - 1)]
     peers += [at((ctx + o) % n_ctx, plane, z) for o in range(1, n_ctx)]
     for peer in peers:
         pl.semaphore_signal(barrier, inc=1, device_id=peer, device_id_type=MESH)
@@ -116,9 +128,6 @@
             send_sem=rs_send.at[k, slot], recv_sem=rs_recv.at[k, slot],
             device_id=target, device_id_type=MESH,
         )
-
-    def toward(position):
-        return position - 1 if position > 0 else position + 1
 
     loads[0].wait()
     loads[1].wait()
@@ -138,7 +147,7 @@
 
     def send_gather(k, kind, position):
         if kind == "o":
-            source = toward(position)
+            source = GATHER_OWN[k][position]
             if source:
                 need(k, "o", source)
             gather_copy(k, "o", position, "o", source, at(ctx, plane, ring_at(k, position - source))).start()
@@ -151,7 +160,7 @@
             need(k, "t", source)
             gather_copy(k, "t", position, "t", source, at(ctx, plane, ring_at(k, position - source))).start()
 
-    first_wait = next(i for i, (k, kind, p) in enumerate(GATHER_ORDER) if (kind, p) not in (("o", 1), ("o", -1), ("t", 0)))
+    first_wait = next(i for i, (k, kind, p) in enumerate(GATHER_ORDER) if (kind, p) != ("t", 0) and (kind != "o" or GATHER_OWN[k][p]))
     for step in GATHER_ORDER[:first_wait]:
         send_gather(*step)
 
@@ -332,7 +341,7 @@
     def terms_of(k, kind, position):
         terms = [("t", p) for p in STEPS if kind == "t" and SCATTER_TO[k][p] == position]
         if kind == "o":
-            terms += [("o", p) for p in STEPS if toward(p) == position]
+            terms += [("o", p) for p in STEPS if SCATTER_OWN[k][p] == position]
             terms += [("t", position)] if SCATTER_TO[k][position] == "x" else []
         return terms
 
@@ -341,11 +350,9 @@
         if terms:
             mine, total = add(k, kind, position, terms)
             part[k, mine, :] = total.astype(jnp.bfloat16)
-        target = toward(position) if kind == "o" else SCATTER_TO[k][position]
+        target = (SCATTER_OWN if kind == "o" else SCATTER_TO)[k][position]
         device = partner if target == "x" else at(ctx, plane, ring_at(k, target - position))
         scatter_copy(k, kind, position, device).start()
-
-    late = (("t", 0), ("o", 1), ("o", -1))
 
     def drain(k, kinds):
         for kind, position in kinds:
@@ -358,13 +365,13 @@
             product = jnp.dot(gated[...], wout[:, columns], preferred_element_type=jnp.float32)
             part[k] = product.astype(jnp.bfloat16)
         elif kind == "F":
-            drain(k, [other for other in SLOT if other not in late])
+            drain(k, [other for other in SLOT if other not in terms_of(k, "o", 0)])
             _, total = add(k, "o", 0, terms_of(k, "o", 0))
             out[:, columns] = (total + tok[:, columns].astype(jnp.float32)).astype(jnp.bfloat16)
         else:
             send_scatter(k, kind, position)
     for k in range(SLICES):
-        drain(k, late)
+        drain(k, terms_of(k, "o", 0))
     for copy in copies:
         copy.wait_send()
 

time: 58.8 us -> 57.5 us (0.978)
  Pallas kernels: 57.5 us -> 56.6 us
    pallas_call x1, Pallas kernels: 57.5 us -> 56.6 us  [on_device(): pl.pallas_call(functools.partial(kernel, (ring, n_ctx, rows, width)), out...]
where the time goes in v5:
time: 57.5 us; the launch traced here: 57.2 us
  Pallas kernels  56.6 us (98%)
  local copies, waits for them, and re-layouts  0.66 us (1%)
    pallas_call x1, Pallas kernels, on_device(): pl.pallas_call(functools.partial(kernel, (ring, n_ctx, rows, width)), out...  56.6 us

profile of v5, /device:TPU:2, one launch (start us, length us, event | category | flops | bytes accessed | tf_op | source)
XLA Modules:
  0.0 57.2 jit_solution(11379713471789184439)
XLA Ops:
  0.0 56.6 %hyena_layer.1 = bf16[16,4096]{1,0:T(8,128)(2,1)S(1)} custom-call(bf16[16,4096]{1,0:T(8,128)(2,1)} %tokens_hbm.1, f32[1,4096]{1,0:T(1,128)} %bitcast.4, bf16[3,4096,256]{2,1,0:T(8,128)(2,1)} %bitcast.3, bf16[3,3,256]{2,1,0:T(4,128)(2,1)} %taps_hbm.1, f32[16,256]{1,0:T(8,128)} %res_hbm.1, f32[16,256]{1,0:T(8,128)} %rate_hbm.1, f32[1,256]{1,0:T(1,128)} %bitcast.5, ...), custom_call_target="tpu_custom_call" | custom-call | flops 2147483648 | bytes 8388608 | tf_op jit(solution)/shard_map/hyena_layer/pallas_call | solution.py:389
  56.6 0.7 %copy.10 = bf16[16,4096]{1,0:T(8,128)(2,1)} copy(bf16[16,4096]{1,0:T(8,128)(2,1)S(1)} %hyena_layer.1) | data formatting | bytes 262144

commit v6 on v5

--- a/solution.py
+++ b/solution.py
@@ -98,6 +98,7 @@
     for load in loads:
         load.start()
 
+    messages[...] = jnp.zeros(messages.shape, messages.dtype)
     barrier = pltpu.get_barrier_semaphore()
     peers = [partner] + [at(ctx, plane, (z + steps) % ring) for steps in (1, 2, ring - 2, ring - 1)]
     peers += [at((ctx + o) % n_ctx, plane, z) for o in range(1, n_ctx)]
@@ -222,7 +223,7 @@
         short_mix(i, proj[:, i, :], proj[:, i - 1, :], proj[:, i - 2, :])
         return carry
 
-    lax.fori_loop(2, seg, short_step, 0, unroll=6)
+    lax.fori_loop(2, seg, short_step, 0, unroll=True)
 
     first_row = lax.broadcasted_iota(jnp.int32, (SEGMENTS, 3 * channels), 0) == 0
     first_sig = lax.broadcasted_iota(jnp.int32, (SEGMENTS, channels), 0) == 0
@@ -241,7 +242,7 @@
         def end_step(i, carry, half=half):
             return dec[:, :, half] * carry + sig[i, :, half][None]
 
-        total = lax.fori_loop(0, seg, end_step, jnp.zeros((modes, SEGMENTS, 128), jnp.float32), unroll=8)
+        total = lax.fori_loop(0, seg, end_step, jnp.zeros((modes, SEGMENTS, 128), jnp.float32), unroll=True)
         leap = far[:, :, half]
         for hop in (1, 2, 4):
             total = total + jnp.where(lane >= hop, leap * pltpu.roll(total, hop, 1), 0.0)
@@ -265,8 +266,12 @@
         )
         for o in range(1, n_ctx)
     ]
-    for copy in copies:
-        copy.start()
+    for o, copy in enumerate(copies, 1):
+
+        @pl.when(ctx + o < n_ctx)
+        def _(copy=copy):
+            copy.start()
+
 
     for half in halves:
         ends[:, :, half] = jnp.where(lane >= 1, pltpu.roll(ends[:, :, half], 1, 1), 0.0)
@@ -276,8 +281,12 @@
             gather_copy(k, kind, position, kind, position, partner).wait_send()
 
     for o in range(1, n_ctx):
-        copies[o - 1].wait_recv()
-        before[o - 1] = jnp.where(o <= ctx, messages[o - 1, modes:, :].astype(jnp.float32), 0.0)
+
+        @pl.when(o <= ctx)
+        def _(o=o):
+            copies[o - 1].wait_recv()
+
+        before[o - 1] = messages[o - 1, modes:, :].astype(jnp.float32)
     before[n_ctx - 1] = jnp.zeros(before.shape[1:], jnp.float32)
     before[n_ctx] = jnp.zeros(before.shape[1:], jnp.float32)
 
@@ -295,7 +304,7 @@
     decay = decays[0]
     incoming = jnp.zeros(rate.shape, jnp.float32)
     for o in range(n_ctx - 1, 0, -1):
-        ended = jnp.where(o <= ctx, messages[o - 1, 0:modes, :].astype(jnp.float32), 0.0)
+        ended = messages[o - 1, 0:modes, :].astype(jnp.float32)
         head = decay * heads[0, o - 1 : o, :] + heads[1, o - 1 : o, :]
         incoming = decays[1] * incoming + (ended + decays[2] * head)
 
@@ -323,7 +332,7 @@
             gated32[i, :, half] = gate[i, :, half] * (mixed + skip[:, half] * now)
             return carry
 
-        lax.fori_loop(0, seg, long_step, ends[:, :, half], unroll=4)
+        lax.fori_loop(0, seg, long_step, ends[:, :, half], unroll=True)
     for s in range(SEGMENTS):
         gated[s * seg : (s + 1) * seg, :] = gated32[:, s, :].astype(jnp.bfloat16)
 
@@ -372,8 +381,11 @@
             send_scatter(k, kind, position)
     for k in range(SLICES):
         drain(k, terms_of(k, "o", 0))
-    for copy in copies:
-        copy.wait_send()
+    for o, copy in enumerate(copies, 1):
+
+        @pl.when(ctx + o < n_ctx)
+        def _(copy=copy):
+            copy.wait_send()
 
 
 def on_device(ring, n_ctx, tokens, norm_gain, in_weight, short_filter, residues, decay_rate, skip_gain, out_weight):

time: 57.5 us -> 56.5 us (0.983)
  Pallas kernels: 56.6 us -> 55.5 us
    pallas_call x1, Pallas kernels: 56.6 us -> 55.5 us  [on_device(): pl.pallas_call(functools.partial(kernel, (ring, n_ctx, rows, width)), out...]
where the time goes in v6:
time: 56.5 us; the launch traced here: 56.1 us
  Pallas kernels  55.5 us (98%)
  local copies, waits for them, and re-layouts  0.66 us (1%)
    pallas_call x1, Pallas kernels, on_device(): pl.pallas_call(functools.partial(kernel, (ring, n_ctx, rows, width)), out...  55.5 us

profile of v6, /device:TPU:2, one launch (start us, length us, event | category | flops | bytes accessed | tf_op | source)
XLA Modules:
  0.0 56.1 jit_solution(3733300090204343126)
XLA Ops:
  0.0 55.5 %hyena_layer.1 = bf16[16,4096]{1,0:T(8,128)(2,1)S(1)} custom-call(bf16[16,4096]{1,0:T(8,128)(2,1)} %tokens_hbm.1, f32[1,4096]{1,0:T(1,128)} %bitcast.4, bf16[3,4096,256]{2,1,0:T(8,128)(2,1)} %bitcast.3, bf16[3,3,256]{2,1,0:T(4,128)(2,1)} %taps_hbm.1, f32[16,256]{1,0:T(8,128)} %res_hbm.1, f32[16,256]{1,0:T(8,128)} %rate_hbm.1, f32[1,256]{1,0:T(1,128)} %bitcast.5, ...), custom_call_target="tpu_custom_call" | custom-call | flops 2147483648 | bytes 8388608 | tf_op jit(solution)/shard_map/hyena_layer/pallas_call | solution.py:401
  55.5 0.7 %copy.10 = bf16[16,4096]{1,0:T(8,128)(2,1)} copy(bf16[16,4096]{1,0:T(8,128)(2,1)S(1)} %hyena_layer.1) | data formatting | bytes 262144

commit v7 on v6

--- a/solution.py
+++ b/solution.py
@@ -13,10 +13,10 @@
 SEGMENTS = 8
 STEPS = (1, 2, 3, 4, -1, -2, -3)
 GATHER_FROM = (
-    {-3: -2, -2: "x", -1: 0, 0: "x", 1: 2, 2: "x", 3: "x", 4: 3},
-    {-3: -2, -2: -1, -1: 0, 0: "x", 1: "x", 2: "x", 3: "x", 4: "x"},
-    {-3: "x", -2: "x", -1: 0, 0: "x", 1: 0, 2: 3, 3: "x", 4: 3},
-    {-3: "x", -2: "x", -1: "x", 0: "x", 1: 2, 2: "x", 3: "x", 4: 3},
+    {-3: -2, -2: "x", -1: "x", 0: "x", 1: "x", 2: 1, 3: "x", 4: "x"},
+    {-3: -2, -2: "x", -1: -2, 0: "x", 1: "x", 2: 1, 3: "x", 4: "x"},
+    {-3: -2, -2: "x", -1: "x", 0: "x", 1: 0, 2: "x", 3: "x", 4: 3},
+    {-3: -2, -2: "x", -1: 0, 0: "x", 1: "x", 2: "x", 3: 1, 4: 3},
 )
 SCATTER_TO = (
     {-3: -2, -2: -1, -1: "x", 0: "x", 1: "x", 2: 1, 3: "x", 4: 3},
@@ -25,10 +25,10 @@
     {-3: -2, -2: -1, -1: "x", 0: "x", 1: 0, 2: "x", 3: "x", 4: "x"},
 )
 GATHER_OWN = (
-    {1: 0, 2: 0, 3: 2, 4: 3, -1: 0, -2: 0, -3: -2},
-    {1: 0, 2: 1, 3: 2, 4: 2, -1: 0, -2: -1, -3: -2},
-    {1: 0, 2: 0, 3: 2, 4: 3, -1: 0, -2: -1, -3: -2},
-    {1: 0, 2: 0, 3: 2, 4: 3, -1: 0, -2: -1, -3: -2},
+    {1: 0, 2: 1, 3: 1, 4: 3, -1: 0, -2: -1, -3: -2},
+    {1: 0, 2: 1, 3: 1, 4: 3, -1: 0, -2: 0, -3: -2},
+    {1: 0, 2: 1, 3: 2, 4: 3, -1: 0, -2: 0, -3: -2},
+    {1: 0, 2: 1, 3: 2, 4: 3, -1: 0, -2: 0, -3: -2},
 )
 SCATTER_OWN = (
     {1: 0, 2: 1, 3: 1, 4: 3, -1: 0, -2: -1, -3: -2},
@@ -37,15 +37,15 @@
     {1: 0, 2: 0, 3: 2, 4: 3, -1: 0, -2: -1, -3: -2},
 )
 GATHER_ORDER = (
-    (3, "o", -1), (3, "o", 2), (2, "o", 2), (2, "t", 0), (0, "o", 2), (1, "t", 0), (1, "o", -1), (1, "o", 1),
-    (3, "t", 0), (2, "o", -1), (0, "o", -2), (3, "t", -1), (3, "t", 2), (0, "t", 0), (3, "o", -2),
-    (3, "o", 3), (1, "t", 1), (2, "o", 3), (1, "t", -1), (1, "o", 2), (2, "o", -2), (0, "o", 3), (3, "o", 1),
-    (0, "t", 2), (3, "o", -3), (2, "t", 1), (2, "t", -1), (0, "t", -2), (1, "o", -2), (3, "t", 3),
-    (1, "o", 4), (1, "t", 2), (2, "o", -3), (1, "o", 3), (0, "o", 1), (1, "t", -2), (2, "t", 3), (0, "t", 3),
-    (1, "o", -3), (3, "t", -2), (3, "t", -3), (3, "t", 4), (1, "t", 4), (3, "t", 1), (3, "o", 4),
-    (1, "t", -3), (2, "t", 2), (0, "o", -1), (0, "t", -1), (0, "o", -3), (1, "t", 3), (2, "t", -2),
-    (2, "o", 1), (2, "t", -3), (2, "o", 4), (2, "t", 4), (0, "t", 1), (0, "o", 4), (0, "t", 4), (0, "t", -3),
-    (3, "P", 0), (1, "P", 0), (2, "P", 0), (0, "P", 0),
+    (0, "o", 1), (0, "o", -1), (3, "o", 1), (1, "t", 0), (2, "o", 1), (1, "o", 1), (3, "o", -2), (3, "t", 0),
+    (1, "o", -2), (0, "t", 0), (2, "o", -2), (2, "t", 0), (0, "t", -1), (3, "o", 2), (0, "o", -2),
+    (3, "t", 1), (2, "o", 2), (1, "t", 1), (0, "t", 1), (1, "o", 3), (0, "o", 3), (3, "t", -2), (0, "o", 2),
+    (2, "o", -1), (1, "t", -2), (1, "o", 2), (3, "t", -1), (3, "t", 3), (2, "o", 3), (3, "o", 3),
+    (0, "t", -2), (3, "o", -3), (1, "o", 4), (0, "t", 3), (3, "o", -1), (0, "o", 4), (2, "t", -2),
+    (3, "t", -3), (2, "t", 2), (1, "t", -3), (2, "t", 3), (3, "t", 4), (1, "o", -1), (3, "o", 4),
+    (1, "t", 2), (1, "t", -1), (3, "t", 2), (1, "t", 3), (1, "o", -3), (0, "o", -3), (0, "t", -3),
+    (1, "t", 4), (2, "o", 4), (2, "o", -3), (0, "t", 4), (0, "t", 2), (2, "t", -1), (2, "t", -3),
+    (2, "t", 1), (2, "t", 4), (3, "P", 0), (1, "P", 0), (0, "P", 0), (2, "P", 0),
 )
 SCATTER_ORDER = (
     (2, "M", 0), (2, "t", -1), (2, "o", 4), (2, "t", 4), (2, "t", -3), (1, "M", 0), (1, "t", 4), (3, "M", 0),

time: 56.5 us -> 55.8 us (0.988)
  Pallas kernels: 55.5 us -> 54.7 us
    pallas_call x1, Pallas kernels: 55.5 us -> 54.7 us  [on_device(): pl.pallas_call(functools.partial(kernel, (ring, n_ctx, rows, width)), out...]
where the time goes in v7:
time: 55.8 us; the launch traced here: 55.4 us
  Pallas kernels  54.7 us (98%)
  local copies, waits for them, and re-layouts  0.66 us (1%)
    pallas_call x1, Pallas kernels, on_device(): pl.pallas_call(functools.partial(kernel, (ring, n_ctx, rows, width)), out...  54.7 us

profile of v7, /device:TPU:2, one launch (start us, length us, event | category | flops | bytes accessed | tf_op | source)
XLA Modules:
  0.0 55.4 jit_solution(13315354140893423936)
XLA Ops:
  0.0 54.7 %hyena_layer.1 = bf16[16,4096]{1,0:T(8,128)(2,1)S(1)} custom-call(bf16[16,4096]{1,0:T(8,128)(2,1)} %tokens_hbm.1, f32[1,4096]{1,0:T(1,128)} %bitcast.4, bf16[3,4096,256]{2,1,0:T(8,128)(2,1)} %bitcast.3, bf16[3,3,256]{2,1,0:T(4,128)(2,1)} %taps_hbm.1, f32[16,256]{1,0:T(8,128)} %res_hbm.1, f32[16,256]{1,0:T(8,128)} %rate_hbm.1, f32[1,256]{1,0:T(1,128)} %bitcast.5, ...), custom_call_target="tpu_custom_call" | custom-call | flops 2147483648 | bytes 8388608 | tf_op jit(solution)/shard_map/hyena_layer/pallas_call | solution.py:401
  54.7 0.7 %copy.10 = bf16[16,4096]{1,0:T(8,128)(2,1)} copy(bf16[16,4096]{1,0:T(8,128)(2,1)S(1)} %hyena_layer.1) | data formatting | bytes 262144
